TPU v7x, 32 devices: a whole 2x2x4 slice. The times are simulated.
32 devices in a mesh: dp: 32 (over z, y, x, core).
Axes of the slice: x: 2, y: 2, z: 4, core: 2. Of those that a mesh axis runs over, the one named last changes fastest.
Arguments:
- fields: bfloat16 [32, 4, 1024, 384], P('dp'), may hold values from -6 to 6
- conditions: bfloat16 [32, 4, 384], P('dp'), may hold values from -6 to 6
- step_counts: int32 [32], P('dp'), may hold values from 1 to 4, as said below
- cotangent: bfloat16 [32, 4, 1024, 384], P('dp'), may hold values from -6 to 6
- w_ada: bfloat16 [384, 2304], P('dp'), may hold values from -0.15625 to 0.15625
- b_ada: bfloat16 [2304], P('dp'), may hold values from -3 to 3
- w_qkv: bfloat16 [384, 1152], P('dp'), may hold values from -0.3125 to 0.3125
- w_out: bfloat16 [384, 384], P('dp'), may hold values from -1.25 to 1.25
- b_out: bfloat16 [384], P('dp'), may hold values from -2 to 2
- w_up: bfloat16 [384, 1536], P('dp'), may hold values from -0.3125 to 0.3125
- b_up: bfloat16 [1536], P('dp'), may hold values from -3 to 3
- w_down: bfloat16 [1536, 384], P('dp'), may hold values from -0.15625 to 0.15625
- b_down: bfloat16 [384], P('dp'), may hold values from -2 to 2
Outputs:
- layer_output: bfloat16 [32, 4, 1024, 384], P('dp')
- field_grad: float32 [32, 4, 1024, 384], P('dp')
- grad_w_ada: float32 [384, 2304], P('dp')
- grad_b_ada: float32 [2304], P('dp')
- grad_w_qkv: float32 [384, 1152], P('dp')
- grad_w_out: float32 [384, 384], P('dp')
- grad_b_out: float32 [384], P('dp')
- grad_w_up: float32 [384, 1536], P('dp')
- grad_b_up: float32 [1536], P('dp')
- grad_w_down: float32 [1536, 384], P('dp')
- grad_b_down: float32 [384], P('dp')
Inputs may be any that keep to these rules, and one draw needn't show every extreme that they name: `step_counts`: each item has at least one step; some item has 4 steps and some item has one.
All inputs are finite; a program needn't handle non-finite values.
Results may differ from a plain program's by a relative error of at most 0.02.
Values may be sent and summed in bfloat16 or wider, within the bound.
No kernel may reach another device: no remote copies, remote signals or barrier semaphores. Data moves between devices by JAX's collectives and lax.ppermute only.
A program may use at most 192 MiB of HBM per device.

v0:
```python
import jax
import jax.numpy as jnp
from jax import lax
from jax.sharding import PartitionSpec as P

HEADS = 6
HEAD = 64
QBLOCK = 512


eps = 1e-06
highest = lax.Precision.HIGHEST


def from_partner(block, axis, stride):
    count = lax.axis_size(axis)
    route = []
    for low in range(count):
        high = low | 1 << stride
        if high != low and high < count:
            route += [(low, high), (high, low)]
    return lax.ppermute(block, axis, route)


def norm_parts(value):
    mean = jnp.mean(value, -1, keepdims=True)
    cent = value - mean
    var = jnp.mean(cent * cent, -1, keepdims=True)
    rstd = lax.rsqrt(var + eps)
    return (cent * rstd, rstd)


def norm_backward_pass(grad_n, normed, rstd):
    return rstd * (
        grad_n
        - jnp.mean(grad_n, -1, keepdims=True)
        - normed * jnp.mean(grad_n * normed, -1, keepdims=True)
    )


def block_scores(query_blk, keys):
    return jnp.einsum("bhe,lhe->hbl", query_blk, keys, preferred_element_type=jnp.float32) * 0.125


def attend_forward(query_blk, keys, values):
    scores = block_scores(query_blk, keys)
    top = jnp.max(scores, -1, keepdims=True)
    expo = jnp.exp(scores - top)
    total = jnp.sum(expo, -1, keepdims=True)
    probs = (expo / total).astype(jnp.bfloat16)
    out = jnp.einsum("hbl,lhe->bhe", probs, values, preferred_element_type=jnp.float32)
    return (out, top, total)


def attend_backward(query_blk, grad_blk, top, total, keys, values):
    scores = block_scores(query_blk, keys)
    probs = jnp.exp(scores - top) / total
    probs_low = probs.astype(jnp.bfloat16)
    grad_v = jnp.einsum("hbl,bhe->lhe", probs_low, grad_blk, preferred_element_type=jnp.float32)
    grad_p = jnp.einsum("bhe,lhe->hbl", grad_blk, values, preferred_element_type=jnp.float32)
    delta = jnp.sum(grad_p * probs, -1, keepdims=True)
    grad_s = (probs * (grad_p - delta)).astype(jnp.bfloat16)
    grad_q = jnp.einsum("hbl,lhe->bhe", grad_s, keys, preferred_element_type=jnp.float32) * 0.125
    grad_k = (
        jnp.einsum("hbl,bhe->lhe", grad_s, query_blk, preferred_element_type=jnp.float32) * 0.125
    )
    return (grad_q, grad_k, grad_v)


def rows_t(left, right):
    return jnp.einsum("lm,ln->mn", left, right, preferred_element_type=jnp.float32)


def back_t(grad, weight):
    return jnp.einsum("ln,mn->lm", grad, weight, preferred_element_type=jnp.float32)


def body(
    fields,
    conditions,
    step_counts,
    cotangent,
    w_ada,
    b_ada,
    w_qkv,
    w_out,
    b_out,
    w_up,
    b_up,
    w_down,
    b_down,
):
    gathered = (
        lax.all_gather(w_ada, "dp", axis=0, tiled=True),
        lax.all_gather(b_ada, "dp", axis=0, tiled=True),
        lax.all_gather(w_qkv, "dp", axis=0, tiled=True),
        lax.all_gather(w_out, "dp", axis=0, tiled=True),
        lax.all_gather(b_out, "dp", axis=0, tiled=True),
        lax.all_gather(w_up, "dp", axis=0, tiled=True),
        lax.all_gather(b_up, "dp", axis=0, tiled=True),
        lax.all_gather(w_down, "dp", axis=0, tiled=True),
        lax.all_gather(b_down, "dp", axis=0, tiled=True),
    )
    full_ada, bias_ada, full_qkv, full_out, bias_out, full_up, bias_up, full_down, bias_down = (
        gathered
    )
    own_half = lax.axis_index("dp") % 2
    is_lower = own_half == 0
    steps_all = fields.shape[1]
    length = fields.shape[2]
    width = fields.shape[3]
    half_width = width // 2
    heads_half = HEADS // 2
    ff_half = full_up.shape[1] // 2
    blocks = length // QBLOCK
    counts_wire = step_counts.astype(jnp.bfloat16)
    other_f, other_c, other_g, other_n = from_partner(
        (fields, conditions, cotangent, counts_wire), "dp", 0
    )

    def paired(mine, theirs):
        return jnp.concatenate(
            [jnp.where(is_lower, mine, theirs), jnp.where(is_lower, theirs, mine)], 0
        )

    pair_fields = paired(fields, other_f).reshape(2 * steps_all, length, width)
    pair_conds = paired(conditions, other_c)
    pair_cotan = paired(cotangent, other_g).reshape(2 * steps_all, length, width)
    pair_counts = paired(step_counts, other_n.astype(jnp.int32))
    flat_alive_mask = (
        (jnp.arange(steps_all, dtype=jnp.int32)[None, :] < pair_counts[:, None])
        .astype(jnp.float32)
        .reshape(-1)
    )
    qkv_half = lax.dynamic_index_in_dim(
        full_qkv.reshape(width, 3, 2, half_width), own_half, 2, keepdims=False
    ).reshape(width, 3 * half_width)
    out_half = lax.dynamic_slice_in_dim(full_out, own_half * half_width, half_width, 0)
    up_half = lax.dynamic_slice_in_dim(full_up, own_half * ff_half, ff_half, 1)
    bup_half = lax.dynamic_slice_in_dim(bias_up, own_half * ff_half, ff_half, 0).astype(jnp.float32)
    down_half = lax.dynamic_slice_in_dim(full_down, own_half * ff_half, ff_half, 0)
    ada_half = lax.dynamic_slice_in_dim(full_ada, own_half * 3 * width, 3 * width, 1)
    bada_half = lax.dynamic_slice_in_dim(bias_ada, own_half * 3 * width, 3 * width, 0).astype(
        jnp.float32
    )
    cond_act = jax.nn.silu(pair_conds.astype(jnp.float32)).astype(jnp.bfloat16)
    mod_mine = (
        jnp.einsum("ism,mn->isn", cond_act, ada_half, preferred_element_type=jnp.float32)
        + bada_half
    )
    mod_other = from_partner(mod_mine.astype(jnp.bfloat16), "dp", 0).astype(mod_mine.dtype)
    modul_all = jnp.concatenate(
        [jnp.where(is_lower, mod_mine, mod_other), jnp.where(is_lower, mod_other, mod_mine)], -1
    )
    modul_all = modul_all.reshape(2 * steps_all, 6 * width)
    cond_flat = cond_act.reshape(2 * steps_all, width)

    def step_fn(item_position_index, state):
        out_buf, grad_buf, modgrad_buf, sums = state
        alive_step_mask = flat_alive_mask[item_position_index]
        field = lax.dynamic_index_in_dim(
            pair_fields, item_position_index, 0, keepdims=False
        ).astype(jnp.float32)
        grad_out = (
            lax.dynamic_index_in_dim(pair_cotan, item_position_index, 0, keepdims=False).astype(
                jnp.float32
            )
            * alive_step_mask
        )
        modul = lax.dynamic_index_in_dim(modul_all, item_position_index, 0, keepdims=False)
        shift1, first_scale_vector, gate1, shift2, scale2, second_gate_vector = jnp.split(modul, 6)
        first_normed_input, first_inverse_deviation = norm_parts(field)
        h_first = (first_normed_input * (1.0 + first_scale_vector) + shift1).astype(jnp.bfloat16)
        qkv = jnp.dot(h_first, qkv_half, preferred_element_type=jnp.float32).astype(jnp.bfloat16)
        query = qkv[:, :half_width].reshape(blocks, QBLOCK, heads_half, HEAD)
        keys = qkv[:, half_width : 2 * half_width].reshape(length, heads_half, HEAD)
        values = qkv[:, 2 * half_width :].reshape(length, heads_half, HEAD)
        attended, tops, totals = lax.map(lambda blk: attend_forward(blk, keys, values), query)
        attended = attended.reshape(length, half_width).astype(jnp.bfloat16)
        part_one = jnp.dot(attended, out_half, preferred_element_type=jnp.float32)
        branch1 = (
            part_one
            + from_partner(part_one.astype(jnp.bfloat16), "dp", 0).astype(part_one.dtype)
            + bias_out.astype(jnp.float32)
        )
        middle_residual_state = field + gate1 * branch1
        normed2, rstd2 = norm_parts(middle_residual_state)
        h_second = (normed2 * (1.0 + scale2) + shift2).astype(jnp.bfloat16)
        pre = jnp.dot(h_second, up_half, preferred_element_type=jnp.float32) + bup_half
        gelu_val, gelu_pull = jax.vjp(lambda t: jax.nn.gelu(t, approximate=False), pre)
        hidden = gelu_val.astype(jnp.bfloat16)
        part_two = jnp.dot(hidden, down_half, preferred_element_type=jnp.float32)
        second_branch_output = (
            part_two
            + from_partner(part_two.astype(jnp.bfloat16), "dp", 0).astype(part_two.dtype)
            + bias_down.astype(jnp.float32)
        )
        layer_result_output = (
            (middle_residual_state + second_gate_vector * second_branch_output) * alive_step_mask
        ).astype(jnp.bfloat16)
        grad_b2 = (second_gate_vector * grad_out).astype(jnp.bfloat16)
        grad_gate2 = jnp.sum(grad_out * second_branch_output, 0)
        grad_hidden = back_t(grad_b2, down_half)
        grad_pre = gelu_pull(grad_hidden)[0].astype(jnp.bfloat16)
        part_h2 = back_t(grad_pre, up_half)
        grad_h2 = part_h2 + from_partner(part_h2.astype(jnp.bfloat16), "dp", 0).astype(
            part_h2.dtype
        )
        grad_shift2 = jnp.sum(grad_h2, 0)
        grad_scale2 = jnp.sum(grad_h2 * normed2, 0)
        middle_state_gradient = grad_out + norm_backward_pass(
            grad_h2 * (1.0 + scale2), normed2, rstd2
        )
        grad_b1 = (gate1 * middle_state_gradient).astype(jnp.bfloat16)
        grad_gate1 = jnp.sum(middle_state_gradient * branch1, 0)
        grad_att = back_t(grad_b1, out_half).astype(jnp.bfloat16)
        grad_att_blocks = grad_att.reshape(blocks, QBLOCK, heads_half, HEAD)

        def back_block(carry, inputs):
            acc_k, acc_v = carry
            query_blk, grad_blk, top, total = inputs
            grad_q, grad_k, grad_v = attend_backward(query_blk, grad_blk, top, total, keys, values)
            return ((acc_k + grad_k, acc_v + grad_v), grad_q)

        zero_kv = jnp.zeros((length, heads_half, HEAD), jnp.float32)
        (grad_keys, grad_values), grad_query = lax.scan(
            back_block, (zero_kv, zero_kv), (query, grad_att_blocks, tops, totals)
        )
        grad_qkv = jnp.concatenate(
            [
                grad_query.reshape(length, half_width),
                grad_keys.reshape(length, half_width),
                grad_values.reshape(length, half_width),
            ],
            1,
        ).astype(jnp.bfloat16)
        part_h1 = back_t(grad_qkv, qkv_half)
        first_hidden_gradient = part_h1 + from_partner(
            part_h1.astype(jnp.bfloat16), "dp", 0
        ).astype(part_h1.dtype)
        grad_shift1 = jnp.sum(first_hidden_gradient, 0)
        grad_scale1 = jnp.sum(first_hidden_gradient * first_normed_input, 0)
        field_input_gradient = (
            middle_state_gradient
            + norm_backward_pass(
                first_hidden_gradient * (1.0 + first_scale_vector),
                first_normed_input,
                first_inverse_deviation,
            )
        ) * alive_step_mask
        grad_mod = (
            jnp.concatenate(
                [grad_shift1, grad_scale1, grad_gate1, grad_shift2, grad_scale2, grad_gate2]
            )
            * alive_step_mask
        )
        terms = (
            rows_t(h_first, grad_qkv),
            rows_t(attended, grad_b1),
            jnp.sum(grad_b1.astype(jnp.float32), 0),
            rows_t(h_second, grad_pre),
            jnp.sum(grad_pre.astype(jnp.float32), 0),
            rows_t(hidden, grad_b2),
            jnp.sum(grad_b2.astype(jnp.float32), 0),
        )
        sums = tuple((a + b for a, b in zip(sums, terms)))
        out_buf = lax.dynamic_update_index_in_dim(
            out_buf, layer_result_output, item_position_index, 0
        )
        grad_buf = lax.dynamic_update_index_in_dim(
            grad_buf, field_input_gradient, item_position_index, 0
        )
        modgrad_buf = lax.dynamic_update_index_in_dim(modgrad_buf, grad_mod, item_position_index, 0)
        return (out_buf, grad_buf, modgrad_buf, sums)

    start_sums = (
        jnp.zeros((width, 3 * half_width), jnp.float32),
        jnp.zeros((half_width, width), jnp.float32),
        jnp.zeros((width,), jnp.float32),
        jnp.zeros((width, ff_half), jnp.float32),
        jnp.zeros((ff_half,), jnp.float32),
        jnp.zeros((ff_half, width), jnp.float32),
        jnp.zeros((width,), jnp.float32),
    )
    start = (
        jnp.zeros((2 * steps_all, length, width), jnp.bfloat16),
        jnp.zeros((2 * steps_all, length, width), jnp.float32),
        jnp.zeros((2 * steps_all, 6 * width), jnp.float32),
        start_sums,
    )
    out_buf, grad_buf, modgrad_buf, sums = lax.fori_loop(0, 2 * steps_all, step_fn, start)
    sum_qkv, sum_out, sum_bout, sum_up, sum_bup, sum_down, sum_bdown = sums
    lower_weight = is_lower.astype(jnp.float32)
    place_qkv = lax.dynamic_update_slice_in_dim(
        jnp.zeros((width, 3, 2, half_width), jnp.float32),
        sum_qkv.reshape(width, 3, 1, half_width),
        own_half,
        2,
    ).reshape(width, 3 * width)
    place_out = lax.dynamic_update_slice_in_dim(
        jnp.zeros((width, width), jnp.float32), sum_out, own_half * half_width, 0
    )
    place_up = lax.dynamic_update_slice_in_dim(
        jnp.zeros((width, 2 * ff_half), jnp.float32), sum_up, own_half * ff_half, 1
    )
    place_bup = lax.dynamic_update_slice_in_dim(
        jnp.zeros((2 * ff_half,), jnp.float32), sum_bup, own_half * ff_half, 0
    )
    place_down = lax.dynamic_update_slice_in_dim(
        jnp.zeros((2 * ff_half, width), jnp.float32), sum_down, own_half * ff_half, 0
    )
    block_terms = (
        place_qkv,
        place_out,
        sum_bout * lower_weight,
        place_up,
        place_bup,
        place_down,
        sum_bdown * lower_weight,
    )
    mod_piece = lax.dynamic_slice_in_dim(modgrad_buf, own_half * 3 * width, 3 * width, 1)
    piece_wada = jnp.einsum(
        "sm,sn->mn", cond_flat.astype(jnp.float32), mod_piece, precision=highest
    )
    local_wada = lax.dynamic_update_slice_in_dim(
        jnp.zeros((width, 6 * width), jnp.float32), piece_wada, own_half * 3 * width, 1
    )
    local_bada = lax.dynamic_update_slice_in_dim(
        jnp.zeros((6 * width,), jnp.float32), jnp.sum(mod_piece, 0), own_half * 3 * width, 0
    )
    reduced = lax.psum_scatter(
        (local_wada, local_bada) + block_terms, "dp", scatter_dimension=0, tiled=True
    )
    grad_all = tuple(reduced)
    own_out = lax.dynamic_index_in_dim(
        out_buf.reshape(2, steps_all, length, width), own_half, 0, keepdims=True
    )
    own_grad = lax.dynamic_index_in_dim(
        grad_buf.reshape(2, steps_all, length, width), own_half, 0, keepdims=True
    )
    return (own_out, own_grad) + grad_all


def solution(mesh):
    placed = (
        P("dp", None, None, None),
        P("dp", None, None),
        P("dp"),
        P("dp", None, None, None),
        P("dp", None),
        P("dp"),
        P("dp", None),
        P("dp", None),
        P("dp"),
        P("dp", None),
        P("dp"),
        P("dp", None),
        P("dp"),
    )
    return jax.shard_map(
        body,
        mesh=mesh,
        in_specs=placed,
        out_specs=(
            P("dp", None, None, None),
            P("dp", None, None, None),
            P("dp", None),
            P("dp"),
            P("dp", None),
            P("dp", None),
            P("dp"),
            P("dp", None),
            P("dp"),
            P("dp", None),
            P("dp"),
        ),
        check_vma=False,
    )
```

profile of v0, /device:TPU:0, one launch (start us, length us, event | category | flops | bytes accessed | tf_op | source)
XLA Modules:
  0.0 1362.0 jit_solution(9981877295832996157)
XLA Ops:
  14.7 47.0 %all-gather.1 = bf16[32,12,1152]{2,1,0:T(8,128)(2,1)S(1)} all-gather(bf16[1,12,1152]{2,1,0:T(8,128)(2,1)} %bitcast.307), channel_id=1, replica_groups=mesh['dp'=32] {'dp'}, dimensions={0}, use_global_device_ids=true | all-gather | bytes 912384 | tf_op jit(solution)/shard_map/all_gather | solution.py:96
  67.0 37.8 %all-gather.2 = bf16[32,12,384]{2,1,0:T(8,128)(2,1)S(1)} all-gather(bf16[1,12,384]{2,1,0:T(8,128)(2,1)S(1)} %bitcast.309), channel_id=1, replica_groups=mesh['dp'=32] {'dp'}, dimensions={0}, use_global_device_ids=true | all-gather | bytes 304128 | tf_op jit(solution)/shard_map/all_gather | solution.py:97
  105.9 37.2 %all-reduce.16 = (bf16[2304]{0:T(1024)(128)(2,1)S(1)}, bf16[384]{0:T(512)(128)(2,1)}, bf16[1536]{0:T(1024)(128)(2,1)S(1)}, bf16[384]{0:T(512)(128)(2,1)}) all-reduce(bf16[2304]{0:T(1024)(128)(2,1)S(1)} %dynamic-update-slice, bf16[384]{0:T(512)(128)(2,1)S(1)} %dynamic-update-slice.1, ...), channel_id=1, replica_groups=mesh['dp'=32] {'dp'}, use_global_device_ids=true, to_apply=%add | all-reduce | flops 4608 | bytes 18432
  151.0 7.0 broadcast_select_fusion.1
  161.4 23.3 %all-gather.10.cloned.1.call-done = bf16[32,12,2304]{2,1,0:T(8,128)(2,1)} async-done(((bf16[1,12,2304]{2,1,0:T(8,128)(2,1)}), bf16[32,12,2304]{2,1,0:T(8,128)(2,1)}) %all-gather.10.cloned.1.call-update) | async-done | bytes 1769488 | tf_op jit(solution)/shard_map/all_gather | solution.py:94
  196.1 915.8 %while.105 = (s32[]{:T(128)}, bf16[8,1024,384]{2,1,0:T(8,128)(2,1)}, f32[8,1024,384]{2,1,0:T(8,128)}, f32[8,2304]{1,0:T(8,128)}, f32[384,576]{0,1:T(8,128)}, /*i...) while((s32[]{:T(128)}, bf16[8,1024,384]{2,1,0:T(8,128)(2,1)}, ...), condition=%wide.region_25.26_spmd.clone, body=%wide.region_0.25_spmd.clone.sunk | while | flops 6997771264 | bytes 346388192 | solution.py:291
  226.1 13.6 while.106
  247.6 8.5 multiply_convert_fusion.9
  279.6 29.1 %while.107 = (s32[]{:T(128)}, f32[1024,3,64]{0,2,1:T(8,128)}, f32[1024,3,64]{0,2,1:T(8,128)}, bf16[2,512,3,64]{1,3,2,0:T(8,128)(2,1)}, bf16[2,512,3,64]{1,3,2,0:...) while((s32[]{:T(128)}, f32[1024,3,64]{0,2,1:T(8,128)}, ...), condition=%wide.region_13.13_spmd.clone, body=%wide.region_11.12_spmd.clone.sunk | while | flops 1021868544 | bytes 106217744 | solution.py:226
  337.1 13.6 while.106
  358.6 8.5 multiply_convert_fusion.9
  390.6 29.1 %while.107 = (s32[]{:T(128)}, f32[1024,3,64]{0,2,1:T(8,128)}, f32[1024,3,64]{0,2,1:T(8,128)}, bf16[2,512,3,64]{1,3,2,0:T(8,128)(2,1)}, bf16[2,512,3,64]{1,3,2,0:...) while((s32[]{:T(128)}, f32[1024,3,64]{0,2,1:T(8,128)}, ...), condition=%wide.region_13.13_spmd.clone, body=%wide.region_11.12_spmd.clone.sunk | while | flops 1021868544 | bytes 106217744 | solution.py:226
  448.1 13.6 while.106
  469.6 8.5 multiply_convert_fusion.9
  501.6 29.1 %while.107 = (s32[]{:T(128)}, f32[1024,3,64]{0,2,1:T(8,128)}, f32[1024,3,64]{0,2,1:T(8,128)}, bf16[2,512,3,64]{1,3,2,0:T(8,128)(2,1)}, bf16[2,512,3,64]{1,3,2,0:...) while((s32[]{:T(128)}, f32[1024,3,64]{0,2,1:T(8,128)}, ...), condition=%wide.region_13.13_spmd.clone, body=%wide.region_11.12_spmd.clone.sunk | while | flops 1021868544 | bytes 106217744 | solution.py:226
  559.1 13.6 while.106
  580.6 8.5 multiply_convert_fusion.9
  612.6 29.1 %while.107 = (s32[]{:T(128)}, f32[1024,3,64]{0,2,1:T(8,128)}, f32[1024,3,64]{0,2,1:T(8,128)}, bf16[2,512,3,64]{1,3,2,0:T(8,128)(2,1)}, bf16[2,512,3,64]{1,3,2,0:...) while((s32[]{:T(128)}, f32[1024,3,64]{0,2,1:T(8,128)}, ...), condition=%wide.region_13.13_spmd.clone, body=%wide.region_11.12_spmd.clone.sunk | while | flops 1021868544 | bytes 106217744 | solution.py:226
  670.1 13.6 while.106
  691.6 8.5 multiply_convert_fusion.9
  723.6 29.1 %while.107 = (s32[]{:T(128)}, f32[1024,3,64]{0,2,1:T(8,128)}, f32[1024,3,64]{0,2,1:T(8,128)}, bf16[2,512,3,64]{1,3,2,0:T(8,128)(2,1)}, bf16[2,512,3,64]{1,3,2,0:...) while((s32[]{:T(128)}, f32[1024,3,64]{0,2,1:T(8,128)}, ...), condition=%wide.region_13.13_spmd.clone, body=%wide.region_11.12_spmd.clone.sunk | while | flops 1021868544 | bytes 106217744 | solution.py:226
  781.1 13.6 while.106
  802.6 8.5 multiply_convert_fusion.9
  834.7 29.1 %while.107 = (s32[]{:T(128)}, f32[1024,3,64]{0,2,1:T(8,128)}, f32[1024,3,64]{0,2,1:T(8,128)}, bf16[2,512,3,64]{1,3,2,0:T(8,128)(2,1)}, bf16[2,512,3,64]{1,3,2,0:...) while((s32[]{:T(128)}, f32[1024,3,64]{0,2,1:T(8,128)}, ...), condition=%wide.region_13.13_spmd.clone, body=%wide.region_11.12_spmd.clone.sunk | while | flops 1021868544 | bytes 106217744 | solution.py:226
  892.1 13.6 while.106
  913.6 8.5 multiply_convert_fusion.9
  945.6 29.1 %while.107 = (s32[]{:T(128)}, f32[1024,3,64]{0,2,1:T(8,128)}, f32[1024,3,64]{0,2,1:T(8,128)}, bf16[2,512,3,64]{1,3,2,0:T(8,128)(2,1)}, bf16[2,512,3,64]{1,3,2,0:...) while((s32[]{:T(128)}, f32[1024,3,64]{0,2,1:T(8,128)}, ...), condition=%wide.region_13.13_spmd.clone, body=%wide.region_11.12_spmd.clone.sunk | while | flops 1021868544 | bytes 106217744 | solution.py:226
  1003.1 13.6 while.106
  1024.6 8.5 multiply_convert_fusion.9
  1056.6 29.1 %while.107 = (s32[]{:T(128)}, f32[1024,3,64]{0,2,1:T(8,128)}, f32[1024,3,64]{0,2,1:T(8,128)}, bf16[2,512,3,64]{1,3,2,0:T(8,128)(2,1)}, bf16[2,512,3,64]{1,3,2,0:...) while((s32[]{:T(128)}, f32[1024,3,64]{0,2,1:T(8,128)}, ...), condition=%wide.region_13.13_spmd.clone, body=%wide.region_11.12_spmd.clone.sunk | while | flops 1021868544 | bytes 106217744 | solution.py:226
  1122.1 103.5 %fusion.91 = (f32[16,2304]{1,0:T(8,128)}, f32[16,384]{1,0:T(8,128)}, f32[16,1536]{1,0:T(8,128)}) fusion(f32[384,2304]{1,0:T(8,128)S(1)} %convolution_dynamic-update-slice_fusion, f32[384,384]{1,0:T(8,128)} %copy-done.26, f32[384,1536]{1,0:T(8,128)} %constant_dynamic-update-slice_fusion.7), kind=kCustom, calls=%all-reduce-scatter.3 | all-reduce-scatter fusion | flops 2162689 | bytes 6758400
  1279.1 38.0 %all-reduce.15 = (f32[2304]{0:T(1024)S(1)}, f32[384]{0:T(512)S(1)}, f32[1536]{0:T(1024)S(1)}, f32[384]{0:T(512)S(1)}) all-reduce(f32[2304]{0:T(1024)S(1)} %dynamic_update_slice.60, f32[384]{0:T(512)S(1)} %broadcast_multiply_fusion.8, f32[1536]{0:T(1024)S(1)} %dynamic_update_slice.64, ...), channel_id=3, replica_groups=mesh['dp'=32] {'dp'}, use_global_device_ids=true, to_apply=%region_28.29.clone | all-reduce | flops 4608 | bytes 36864
  (1923 shorter events, 948.4 us)
Async XLA Ops:
  7.2 138.8 %all-gather.12.cloned.1.call-start = ((), (), s32[]{:S(2)}) async-start(), calls=%async_computation.4 | async-start | bytes 1622016 | tf_op jit(solution)/shard_map/all_gather | solution.py:99
  7.9 141.1 %all-gather.8.cloned.1.call-start = ((), (), s32[]{:S(2)}) async-start(), calls=%async_computation.1 | async-start | bytes 1216512 | tf_op jit(solution)/shard_map/all_gather | solution.py:101
  8.7 176.0 %all-gather.10.cloned.1.call-start = ((), (), s32[]{:S(2)}) async-start(), calls=%async_computation.3 | async-start | bytes 2433024 | tf_op jit(solution)/shard_map/all_gather | solution.py:94
  8.7 142.3 %collective-permute-start.8 = (bf16[1,4,1024,384]{3,2,1,0:T(8,128)(2,1)}, bf16[1,4,1024,384]{3,2,1,0:T(8,128)(2,1)}, u32[]{:S(2)}, u32[]{:S(2)}) collective-permute-start(bf16[1,4,1024,384]{3,2,1,0:T(8,128)(2,1)} %param.22), channel_id=1, source_target_pairs={{0,1},{1,0},{2,3},{3,2},{4,5},{5,4},{6,7},{7,6},{8,9},{9,8},{10,11... | collective-permute-start | bytes 9437192 | tf_op jit(solution)/shard_map/ppermute | solution.py:22
  9.2 141.8 %collective-permute-start.4 = (bf16[1,4,1024,384]{3,2,1,0:T(8,128)(2,1)}, bf16[1,4,1024,384]{3,2,1,0:T(8,128)(2,1)}, u32[]{:S(2)}, u32[]{:S(2)}) collective-permute-start(bf16[1,4,1024,384]{3,2,1,0:T(8,128)(2,1)} %param.19), channel_id=1, source_target_pairs={{0,1},{1,0},{2,3},{3,2},{4,5},{5,4},{6,7},{7,6},{8,9},{9,8},{10,11... | collective-permute-start | bytes 9437192 | tf_op jit(solution)/shard_map/ppermute | solution.py:22
  9.4 1341.0 %all-reduce.20.cloned.1.call-start = ((), (), s32[]{:S(2)}) async-start(), calls=%async_computation.5 | async-start | bytes 3538944
  9.4 136.5 %collective-permute-start.5 = (bf16[1,4,384]{2,1,0:T(4,128)(2,1)}, bf16[1,4,384]{2,1,0:T(4,128)(2,1)S(1)}, u32[]{:S(2)}, u32[]{:S(2)}) collective-permute-start(bf16[1,4,384]{2,1,0:T(4,128)(2,1)} %param.20), channel_id=1, source_target_pairs={{0,1},{1,0},{2,3},{3,2},{4,5},{5,4},{6,7},{7,6},{8,9},{9,8},{10,11... | collective-permute-start | bytes 9224 | tf_op jit(solution)/shard_map/ppermute | solution.py:22
  10.6 133.9 %collective-permute-start.7 = (bf16[1]{0:T(256)(128)(2,1)}, bf16[1]{0:T(256)(128)(2,1)}, u32[]{:S(2)}, u32[]{:S(2)}) collective-permute-start(bf16[1]{0:T(256)(128)(2,1)} %convert_element_type.254), channel_id=1, source_target_pairs={{0,1},{1,0},{2,3},{3,2},{4,5},{5,4},{6,7},{7,6},{8,9},{9,8},{10,11... | collective-permute-start | bytes 14 | tf_op jit(solution)/shard_map/ppermute | solution.py:22
  258.2 12.7 collective-permute-start.1
  369.1 12.7 collective-permute-start.1
  591.1 12.7 collective-permute-start.1
  702.2 12.7 collective-permute-start.1
  813.2 12.7 collective-permute-start.1
  924.1 12.7 collective-permute-start.1
  1035.2 12.7 collective-permute-start.1
  1114.4 240.9 %reduce-scatter.9.cloned.1.call-start = ((), (), s32[]{:S(2)}) async-start(), calls=%async_computation.2 | async-start | bytes 2433024 | tf_op jit(solution)/shard_map/reduce_scatter | solution.py:331
  1226.3 23.8 %collective-permute-start.23 = (f32[16,384]{1,0:T(8,128)}, f32[16,384]{1,0:T(8,128)S(1)}, u32[]{:S(2)}, u32[]{:S(2)}) collective-permute-start(f32[16,384]{1,0:T(8,128)} %get-tuple-element.814), channel_id=1, source_target_pairs={{0,7},{1,8},{2,9},{3,10},{4,11},{5,12},{6,13},{7,14},{8,15},{9,16}... | collective-permute-start | bytes 73736
  1227.6 26.0 %collective-permute-start.22 = (f32[16,384]{1,0:T(8,128)}, f32[16,384]{1,0:T(8,128)S(1)}, u32[]{:S(2)}, u32[]{:S(2)}) collective-permute-start(f32[16,384]{1,0:T(8,128)} %get-tuple-element.814), channel_id=1, source_target_pairs={{0,6},{1,7},{2,8},{3,9},{4,10},{5,11},{6,12},{7,13},{8,14},{9,15},... | collective-permute-start | bytes 73736
  1231.3 24.0 %collective-permute-start.21 = (f32[16,384]{1,0:T(8,128)}, f32[16,384]{1,0:T(8,128)S(1)}, u32[]{:S(2)}, u32[]{:S(2)}) collective-permute-start(f32[16,384]{1,0:T(8,128)} %get-tuple-element.814), channel_id=1, source_target_pairs={{0,5},{1,6},{2,7},{3,8},{4,9},{5,10},{6,11},{7,12},{8,13},{9,14},{... | collective-permute-start | bytes 73736
  1236.9 22.9 %collective-permute-start.20 = (f32[16,384]{1,0:T(8,128)}, f32[16,384]{1,0:T(8,128)S(1)}, u32[]{:S(2)}, u32[]{:S(2)}) collective-permute-start(f32[16,384]{1,0:T(8,128)} %get-tuple-element.814), channel_id=1, source_target_pairs={{0,4},{1,5},{2,6},{3,7},{4,8},{5,9},{6,10},{7,11},{8,12},{9,13},{1... | collective-permute-start | bytes 73736
  1248.8 12.9 collective-permute-start.19
  1250.2 12.9 collective-permute-start.18
  1255.3 14.2 %collective-permute-start.31 = (f32[16,1536]{1,0:T(8,128)S(1)}, f32[16,1536]{1,0:T(8,128)S(1)}, u32[]{:S(2)}, u32[]{:S(2)}) collective-permute-start(f32[16,1536]{1,0:T(8,128)S(1)} %copy-done.41), channel_id=1, source_target_pairs={{0,7},{1,8},{2,9},{3,10},{4,11},{5,12},{6,13},{7,14},{8,15},{9,16}... | collective-permute-start | bytes 294920
  1259.8 12.9 collective-permute-start.30
  1263.1 78.1 %collective-permute-start.15 = (f32[16,2304]{1,0:T(8,128)S(1)}, f32[16,2304]{1,0:T(8,128)S(1)}, u32[]{:S(2)}, u32[]{:S(2)}) collective-permute-start(f32[16,2304]{1,0:T(8,128)S(1)} %copy-done.29), channel_id=1, source_target_pairs={{0,7},{1,8},{2,9},{3,10},{4,11},{5,12},{6,13},{7,14},{8,15},{9,16}... | collective-permute-start | bytes 442376
  1265.1 79.3 %collective-permute-start.14 = (f32[16,2304]{1,0:T(8,128)S(1)}, f32[16,2304]{1,0:T(8,128)S(1)}, u32[]{:S(2)}, u32[]{:S(2)}) collective-permute-start(f32[16,2304]{1,0:T(8,128)S(1)} %copy-done.29), channel_id=1, source_target_pairs={{0,6},{1,7},{2,8},{3,9},{4,10},{5,11},{6,12},{7,13},{8,14},{9,15},... | collective-permute-start | bytes 442376
  1267.6 52.8 %collective-permute-start.29 = (f32[16,1536]{1,0:T(8,128)S(1)}, f32[16,1536]{1,0:T(8,128)S(1)}, u32[]{:S(2)}, u32[]{:S(2)}) collective-permute-start(f32[16,1536]{1,0:T(8,128)S(1)} %copy-done.41), channel_id=1, source_target_pairs={{0,5},{1,6},{2,7},{3,8},{4,9},{5,10},{6,11},{7,12},{8,13},{9,14},{... | collective-permute-start | bytes 294920
  1269.6 55.0 %collective-permute-start.28 = (f32[16,1536]{1,0:T(8,128)S(1)}, f32[16,1536]{1,0:T(8,128)S(1)}, u32[]{:S(2)}, u32[]{:S(2)}) collective-permute-start(f32[16,1536]{1,0:T(8,128)S(1)} %copy-done.41), channel_id=1, source_target_pairs={{0,4},{1,5},{2,6},{3,7},{4,8},{5,9},{6,10},{7,11},{8,12},{9,13},{1... | collective-permute-start | bytes 294920
  1272.7 53.2 %collective-permute-start.27 = (f32[16,1536]{1,0:T(8,128)S(1)}, f32[16,1536]{1,0:T(8,128)S(1)}, u32[]{:S(2)}, u32[]{:S(2)}) collective-permute-start(f32[16,1536]{1,0:T(8,128)S(1)} %copy-done.41), channel_id=1, source_target_pairs={{0,3},{1,4},{2,5},{3,6},{4,7},{5,8},{6,9},{7,10},{8,11},{9,12},{10... | collective-permute-start | bytes 294920
  1325.9 13.4 collective-permute-start.16
  1331.2 16.1 %collective-permute-start.13 = (f32[16,2304]{1,0:T(8,128)S(1)}, f32[16,2304]{1,0:T(8,128)S(1)}, u32[]{:S(2)}, u32[]{:S(2)}) collective-permute-start(f32[16,2304]{1,0:T(8,128)S(1)} %copy-done.29), channel_id=1, source_target_pairs={{0,5},{1,6},{2,7},{3,8},{4,9},{5,10},{6,11},{7,12},{8,13},{9,14},{... | collective-permute-start | bytes 442376
  1334.1 13.3 collective-permute-start.12
  (565 other events, 2331.9 us)
Sparse Core Ops, SparseCore 0:
  10.9 58.7 all-gather.11
  72.5 52.9 all-gather.7
  128.4 56.2 all-gather.9
  1114.5 135.5 all-reduce.19
  1255.8 99.3 reduce-scatter.8
where the time goes:
time: 1380 us; the launch traced here: 1360 us
  matrix products  511 us (37%)
  blocking collectives  263 us (19%)
  other arithmetic  249 us (18%)
  local copies, waits for them, and re-layouts  175 us (13%)
  starting transfers between devices  83.7 us (6%)
  loops' own time  35.7 us (3%)
  waiting for transfers between devices  28.3 us (2%)
  between operations  16.2 us (1%)
    unnamed x3, blocking collectives  179 us
    dot_general x32, matrix products, block_scores(): jnp.einsum('bhe,lhe->hbl', query_blk, keys, preferred_element_type=jnp.fl...  74.4 us
    unnamed x25, starting transfers between devices  67.9 us
    dot_general x8, matrix products, step_fn(): jnp.dot(h_second, up_half, preferred_element_type=jnp.float32) + bup_half  67.8 us
    dot_general x32, matrix products, back_t(): jnp.einsum('ln,mn->lm', grad, weight, preferred_element_type=jnp.float32)  67 us
    dot_general x32, matrix products, rows_t(): jnp.einsum('lm,ln->mn', left, right, preferred_element_type=jnp.float32)  57.5 us
    while x1072, local copies, waits for them, and re-layouts  55.1 us
    all_gather x1, blocking collectives, body(): lax.all_gather(w_qkv, 'dp', axis=0, tiled=True)  47 us
  transfers between devices with their start and end apart: 66, of which 3 were waited for; matrix products, arithmetic and copies ran while one was open for 23% of the time, Pallas kernels for 0%

commit v1 on v0

v1 whole, which is shorter than its diff:
```python
import functools
import math

import jax
import jax.numpy as jnp
from jax import lax
from jax.experimental import pallas as pl
from jax.experimental.pallas import tpu as pltpu
from jax.sharding import PartitionSpec as P

HEAD = 64
PAIR = 2 * HEAD
EPS = 1e-6
LOG2E = 1.4426950408889634
VMEM_LIMIT = 60 * 2**20
bf16 = jnp.bfloat16
f32 = jnp.float32


def dot(left, right, left_dim=1, right_dim=0):
    return lax.dot_general(
        left, right, (((left_dim,), (right_dim,)), ((), ())), preferred_element_type=f32
    )


def norm(value):
    mean = jnp.mean(value, -1, keepdims=True)
    cent = value - mean
    var = jnp.mean(cent * cent, -1, keepdims=True)
    rstd = lax.rsqrt(var + EPS)
    return cent * rstd, rstd


def row_sum(value):
    return jnp.sum(value, 0, keepdims=True)


def up_to(value, unit):
    return -(-value // unit) * unit


KEEP, TAKE, CHIP, CORE = range(4)


def is_live(flags, slot, steps):
    return jnp.where(slot < steps, slot < flags[KEEP], flags[TAKE] > 0)


def last_live(flags, slot, steps):
    return jnp.where(is_live(flags, slot, steps), slot, jnp.minimum(slot, flags[KEEP] - 1))


def own_slot(flags, slot):
    return jnp.minimum(slot, flags[KEEP] - 1)


def each_shard(flags, mine_ref, other_ref):
    chips = mine_ref.shape[0]
    first = flags[CORE] == 0
    for chip in range(chips):
        place = jnp.bitwise_xor(flags[CHIP], chip)
        mine = mine_ref[place].astype(f32)
        other = other_ref[place].astype(f32)
        yield 2 * chip, jnp.where(first, mine, other)
        yield 2 * chip + 1, jnp.where(first, other, mine)


def place_columns(dest, device, block, start, rows, count, width):
    for part in range(count):
        dest[device * rows : (device + 1) * rows, part * width : (part + 1) * width] = block[
            start + part * rows : start + (part + 1) * rows
        ]


def attend_forward_body(
    steps, flags, own_x, far_x, cond, mine, other,
    qkv, expo, att, inv, mod, bias, w_f32, w_qkv,
):
    slot = pl.program_id(0)
    pair = pl.program_id(1)
    live = is_live(flags, slot, steps)
    length, width = att.shape[1:]
    devices = 2 * mine.shape[0]
    rows = width // devices

    @pl.when((slot == 0) & (pair == 0))
    def _():
        total = jnp.zeros((12, width), f32)
        for device, block in each_shard(flags, mine, other):
            place_columns(w_f32, device, block, 0, rows, 6, width)
            total = total + block[9 * rows : 9 * rows + 12]
        for part in range(6):
            cols = slice(part * width, (part + 1) * width)
            mod[:, cols] = dot(cond[...], w_f32[:, cols].astype(bf16)) + total[part : part + 1]
            bias[:, cols] = total[6 + part : 7 + part]
        for device, block in each_shard(flags, mine, other):
            place_columns(w_f32, device, block, 6 * rows, rows, 3, width)
        w_qkv[...] = w_f32[:, : 3 * width].astype(bf16)

    row_block = 256

    @pl.when(live & (pair == 0))
    def _():
        shift = mod[pl.ds(slot, 1), :width]
        scale = 1.0 + mod[pl.ds(slot, 1), width : 2 * width]

        def project(ref):
            @pl.loop(0, length // row_block)
            def _(i):
                r = pl.ds(pl.multiple_of(i * row_block, row_block), row_block)
                normed, _ = norm(ref[0, r, :].astype(f32))
                h1 = (normed * scale + shift).astype(bf16)
                qkv[0, r, :] = dot(h1, w_qkv[...]).astype(bf16)

        @pl.when(slot < steps)
        def _():
            project(own_x)

        @pl.when(slot >= steps)
        def _():
            project(far_x)

    @pl.when(live)
    def _():
        c0 = pl.multiple_of(pair * PAIR, PAIR)
        keys = qkv[0, :, pl.ds(pl.multiple_of(width + pair * PAIR, PAIR), PAIR)]
        values = qkv[0, :, pl.ds(pl.multiple_of(2 * width + pair * PAIR, PAIR), PAIR)]
        values_ones = jnp.concatenate([values, jnp.ones_like(values)], 1)
        first = lax.broadcasted_iota(jnp.int32, (row_block, PAIR), 1) < HEAD
        for i in range(length // row_block):
            r = pl.ds(i * row_block, row_block)
            query = qkv[0, r, pl.ds(c0, PAIR)]
            outs = []
            for head in range(2):
                sel = first if head == 0 else jnp.logical_not(first)
                scores = dot(jnp.where(sel, query, jnp.zeros_like(query)), keys, 1, 1)
                top = jnp.max(scores, -1, keepdims=True)
                e = jnp.exp2((scores - top) * (0.125 * LOG2E)).astype(bf16)
                expo[0, head, r, :] = e
                outs.append(dot(e, values_ones))
            out = jnp.where(first, outs[0][:, :PAIR], outs[1][:, :PAIR])
            inverse = 1.0 / jnp.where(first, outs[0][:, PAIR:], outs[1][:, PAIR:])
            att[0, r, pl.ds(c0, PAIR)] = (out * inverse).astype(bf16)
            inv[0, r, pl.ds(c0, PAIR)] = inverse


def attend_forward(flags, own_x, far_x, cond, mine, other):
    steps, length, width = own_x.shape
    slots = steps + 1
    pairs = width // PAIR

    def const(*zeros):
        return lambda s, p, flags: zeros

    def whole(s, p, flags):
        return (last_live(flags, s, steps), 0, 0)

    def expo_at(s, p, flags):
        at = last_live(flags, s, steps)
        return (at, jnp.where(at == s, p, pairs - 1), 0, 0)

    spec = pltpu.PrefetchScalarGridSpec(
        num_scalar_prefetch=1,
        grid=(slots, pairs),
        in_specs=[
            pl.BlockSpec((1, length, width), lambda s, p, flags: (own_slot(flags, s), 0, 0)),
            pl.BlockSpec((1, length, width), const(0, 0, 0)),
            pl.BlockSpec(cond.shape, const(0, 0)),
            pl.BlockSpec(mine.shape, const(0, 0, 0)),
            pl.BlockSpec(other.shape, const(0, 0, 0)),
        ],
        out_specs=[
            pl.BlockSpec((1, length, 3 * width), whole),
            pl.BlockSpec((1, 2, length, length), expo_at),
            pl.BlockSpec((1, length, width), whole),
            pl.BlockSpec((1, length, width), whole),
            pl.BlockSpec((8, 6 * width), const(0, 0)),
            pl.BlockSpec((1, 6 * width), const(0, 0)),
        ],
        scratch_shapes=[
            pltpu.VMEM((width, 6 * width), f32),
            pltpu.VMEM((width, 3 * width), bf16),
        ],
    )
    shape = jax.ShapeDtypeStruct
    return pl.pallas_call(
        functools.partial(attend_forward_body, steps),
        grid_spec=spec,
        out_shape=[
            shape((slots, length, 3 * width), bf16),
            shape((slots, 2 * pairs, length, length), bf16),
            shape((slots, length, width), bf16),
            shape((slots, length, width), f32),
            shape((8, 6 * width), f32),
            shape((1, 6 * width), f32),
        ],
        compiler_params=pltpu.CompilerParams(vmem_limit_bytes=VMEM_LIMIT),
        cost_estimate=pl.CostEstimate(
            flops=6 * 10**9, bytes_accessed=40 * 10**6, transcendentals=2 * 10**7
        ),
        name="attend_forward",
    )(flags, own_x, far_x, cond, mine, other)


def feed_forward_body(
    steps, flags, own_x, far_x, own_g, far_g, att, inv, mod, bias, mine, other,
    own_out, far_out, grad_x1, grad_att, grad_mod, packed, bias_sum,
    x_s, g_s, w_out, w_up, w_down, sum_out, sum_up, sum_down_t, down_f32,
):
    slot = pl.program_id(0)
    step = pl.program_id(1)
    live = is_live(flags, slot, steps)
    width = x_s.shape[1]
    hidden_units = w_up.shape[1]
    ratio = hidden_units // width
    chips = mine.shape[0]
    rows = width // (2 * chips)

    @pl.when((slot == 0) & (step == 0))
    def _():
        for device, block in each_shard(flags, mine, other):
            place_columns(sum_out, device, block, 0, rows, 1, width)
            place_columns(sum_up, device, block, rows, rows, ratio, width)
            place_columns(
                down_f32, device, block, (1 + ratio) * rows, ratio * rows, 1, width
            )
        w_out[...] = sum_out[...].astype(bf16)
        w_up[...] = sum_up[...].astype(bf16)
        w_down[...] = down_f32[...].astype(bf16)
        for ref in (sum_out, sum_up, sum_down_t, bias_sum):
            ref[...] = jnp.zeros_like(ref)

    @pl.when(step == 0)
    def _():
        grad_mod[...] = jnp.zeros_like(grad_mod)

    @pl.when((slot < steps) & jnp.logical_not(live))
    def _():
        own_out[...] = jnp.zeros_like(own_out)

    @pl.when(live)
    def _():
        @pl.when(slot < steps)
        def _():
            x_s[...] = own_x[0].astype(f32)
            g_s[...] = own_g[0].astype(f32)

        @pl.when(slot >= steps)
        def _():
            x_s[...] = far_x[0].astype(f32)
            g_s[...] = far_g[0].astype(f32)

        def vector(part):
            return mod[pl.ds(slot, 1), part * width : (part + 1) * width]

        gate1, shift2, scale2, gate2 = vector(2), vector(3), 1.0 + vector(4), vector(5)
        b_out = bias[:, :width]
        b_up = bias[:, width : width + hidden_units]
        b_down = bias[:, width + hidden_units :]
        attended = att[0]
        branch1 = dot(attended, w_out[...]) + b_out
        x1 = x_s[...] + gate1 * branch1
        normed2, rstd = norm(x1)
        h2 = (normed2 * scale2 + shift2).astype(bf16)
        pre = dot(h2, w_up[...]) + b_up
        cdf = 0.5 * (1.0 + lax.erf(pre * (1 / math.sqrt(2.0))))
        hidden = (pre * cdf).astype(bf16)
        slope = cdf + pre * jnp.exp2(pre * pre * (-0.5 * LOG2E)) * (1 / math.sqrt(2 * math.pi))
        branch2 = dot(hidden, w_down[...]) + b_down
        result = (x1 + gate2 * branch2).astype(bf16)

        @pl.when(slot < steps)
        def _():
            own_out[0] = result

        @pl.when(slot >= steps)
        def _():
            far_out[0] = result

        grad = g_s[...]
        grad_b2 = (gate2 * grad).astype(bf16)
        grad_pre = (dot(grad_b2, w_down[...], 1, 1) * slope).astype(bf16)
        grad_h2 = dot(grad_pre, w_up[...], 1, 1)
        grad_n = grad_h2 * scale2
        g_x1 = grad + rstd * (
            grad_n
            - jnp.mean(grad_n, -1, keepdims=True)
            - normed2 * jnp.mean(grad_n * normed2, -1, keepdims=True)
        )
        grad_b1 = (gate1 * g_x1).astype(bf16)
        grad_x1[0] = g_x1
        grad_att[0] = (dot(grad_b1, w_out[...], 1, 1) * inv[0]).astype(bf16)
        grad_mod[0, 2:3] += row_sum(g_x1 * branch1)
        grad_mod[0, 3:4] += row_sum(grad_h2)
        grad_mod[0, 4:5] += row_sum(grad_h2 * normed2)
        grad_mod[0, 5:6] += row_sum(grad * branch2)
        sum_out[...] += dot(attended, grad_b1, 0, 0)
        sum_up[...] += dot(h2, grad_pre, 0, 0)
        sum_down_t[...] += dot(grad_b2, hidden, 0, 0)
        bias_sum[:, :width] += row_sum(grad_b1.astype(f32))
        bias_sum[:, width : width + hidden_units] += row_sum(grad_pre.astype(f32))
        bias_sum[:, width + hidden_units :] += row_sum(grad_b2.astype(f32))

    @pl.when((slot == steps) & (step == pl.num_programs(1) - 1))
    def _():
        down_f32[...] = sum_down_t[...].T
        for device in range(2 * chips):
            place = (
                jnp.bitwise_xor(flags[CORE], device & 1) * chips
                + jnp.bitwise_xor(flags[CHIP], device >> 1)
            )
            span = slice(device * rows, (device + 1) * rows)
            packed[place, :rows] = sum_out[span]
            for part in range(ratio):
                packed[place, (1 + part) * rows : (2 + part) * rows] = sum_up[
                    span, part * width : (part + 1) * width
                ]
            packed[place, (1 + ratio) * rows : (1 + 2 * ratio) * rows] = down_f32[
                device * ratio * rows : (device + 1) * ratio * rows
            ]


def feed_forward(flags, own_x, far_x, own_g, far_g, att, inv, mod, bias, mine, other, hidden_units):
    steps, length, width = own_x.shape
    slots = steps + 1
    row_block = 512
    blocks = length // row_block
    chips = mine.shape[0]
    rows = width // (2 * chips)
    ratio = hidden_units // width
    packed_rows = up_to((1 + 2 * ratio) * rows, 8)

    def const(*zeros):
        return lambda s, b, flags: zeros

    def own(s, b, flags):
        return (own_slot(flags, s), jnp.where(s < flags[KEEP], b, blocks - 1), 0)

    def far(s, b, flags):
        return (0, jnp.where(s < steps, 0, b), 0)

    def at(s, b, flags):
        live = last_live(flags, s, steps)
        return (live, jnp.where(live == s, b, blocks - 1), 0)

    def own_result(s, b, flags):
        return (jnp.minimum(s, steps - 1), jnp.where(s < steps, b, blocks - 1), 0)

    def block(where):
        return pl.BlockSpec((1, row_block, width), where)

    def fixed(array_shape):
        return pl.BlockSpec(array_shape, const(*[0] * len(array_shape)))

    spec = pltpu.PrefetchScalarGridSpec(
        num_scalar_prefetch=1,
        grid=(slots, blocks),
        in_specs=[
            block(own), block(far), block(own), block(far), block(at), block(at),
            fixed(mod.shape), fixed(bias.shape), fixed(mine.shape), fixed(other.shape),
        ],
        out_specs=[
            block(own_result), block(far), block(at), block(at),
            pl.BlockSpec((1, 8, width), lambda s, b, flags: (s, 0, 0)),
            fixed((2 * chips, packed_rows, width)),
            fixed(bias.shape),
        ],
        scratch_shapes=[
            pltpu.VMEM((row_block, width), f32),
            pltpu.VMEM((row_block, width), f32),
            pltpu.VMEM((width, width), bf16),
            pltpu.VMEM((width, hidden_units), bf16),
            pltpu.VMEM((hidden_units, width), bf16),
            pltpu.VMEM((width, width), f32),
            pltpu.VMEM((width, hidden_units), f32),
            pltpu.VMEM((width, hidden_units), f32),
            pltpu.VMEM((hidden_units, width), f32),
        ],
    )
    shape = jax.ShapeDtypeStruct
    return pl.pallas_call(
        functools.partial(feed_forward_body, steps),
        grid_spec=spec,
        out_shape=[
            shape((steps, length, width), bf16),
            shape((1, length, width), bf16),
            shape((slots, length, width), f32),
            shape((slots, length, width), bf16),
            shape((slots, 8, width), f32),
            shape((2 * chips, packed_rows, width), f32),
            shape(bias.shape, f32),
        ],
        compiler_params=pltpu.CompilerParams(vmem_limit_bytes=VMEM_LIMIT),
        cost_estimate=pl.CostEstimate(
            flops=20 * 10**9, bytes_accessed=40 * 10**6, transcendentals=10**7
        ),
        name="feed_forward",
    )(flags, own_x, far_x, own_g, far_g, att, inv, mod, bias, mine, other)


def attend_backward_body(
    steps, flags, own_x, far_x, qkv, expo, att, grad_att, grad_x1, mod, mine, other,
    own_grad, far_grad, grad_mod, packed, w_f32, w_qkv, g_qkv, keys_t, values_t,
):
    slot = pl.program_id(0)
    pair = pl.program_id(1)
    last_pair = pl.num_programs(1) - 1
    live = is_live(flags, slot, steps)
    length, width = att.shape[1:]
    chips = mine.shape[0]
    rows = width // (2 * chips)
    row_block = 512

    @pl.when((slot == 0) & (pair == 0))
    def _():
        for device, block in each_shard(flags, mine, other):
            place_columns(w_f32, device, block, 6 * rows, rows, 3, width)
        w_qkv[...] = w_f32[...].astype(bf16)
        w_f32[...] = jnp.zeros_like(w_f32)

    @pl.when(pair == 0)
    def _():
        grad_mod[...] = jnp.zeros_like(grad_mod)

    @pl.when((slot < steps) & jnp.logical_not(live))
    def _():
        own_grad[...] = jnp.zeros_like(own_grad)

    @pl.when(live)
    def _():
        c0 = pl.multiple_of(pair * PAIR, PAIR)
        c1 = pl.multiple_of(width + pair * PAIR, PAIR)
        c2 = pl.multiple_of(2 * width + pair * PAIR, PAIR)
        keys = qkv[0, :, pl.ds(c1, PAIR)]
        values = qkv[0, :, pl.ds(c2, PAIR)]
        values_ones = jnp.concatenate([values, jnp.ones_like(values)], 1)
        lane = lax.broadcasted_iota(jnp.int32, (row_block, PAIR), 1)
        first = lane < HEAD
        for i in range(length // row_block):
            r = pl.ds(i * row_block, row_block)
            query = qkv[0, r, pl.ds(c0, PAIR)]
            g_att = grad_att[0, r, pl.ds(c0, PAIR)]
            product = g_att.astype(f32) * att[0, r, pl.ds(c0, PAIR)].astype(f32)
            query_t = query.T
            g_att_t = g_att.T
            grads_q = []
            for head in range(2):
                sel = first if head == 0 else jnp.logical_not(first)
                delta = jnp.sum(jnp.where(sel, product, 0.0), -1, keepdims=True)
                high = delta.astype(bf16).astype(f32)
                extra = jnp.where(
                    lane == 0, -high, jnp.where(lane == 1, high - delta, 0.0)
                ).astype(bf16)
                left = jnp.concatenate([jnp.where(sel, g_att, jnp.zeros_like(g_att)), extra], 1)
                e = expo[0, head, r, :]
                grad_s = e * dot(left, values_ones, 1, 1).astype(bf16)
                grads_q.append(dot(grad_s, keys))
                span = slice(head * HEAD, (head + 1) * HEAD)
                add_k = dot(query_t[span], grad_s)
                add_v = dot(g_att_t[span], e)
                if i == 0:
                    keys_t[span] = add_k
                    values_t[span] = add_v
                else:
                    keys_t[span] += add_k
                    values_t[span] += add_v
            g_qkv[r, pl.ds(c0, PAIR)] = (
                jnp.where(first, grads_q[0], grads_q[1]) * 0.125
            ).astype(bf16)
        g_qkv[:, pl.ds(c1, PAIR)] = (keys_t[...] * 0.125).astype(bf16).T
        g_qkv[:, pl.ds(c2, PAIR)] = values_t[...].astype(bf16).T

    @pl.when(live & (pair == last_pair))
    def _():
        shift = mod[pl.ds(slot, 1), :width]
        scale = 1.0 + mod[pl.ds(slot, 1), width : 2 * width]

        def finish(x_ref, out_ref):
            for i in range(length // row_block):
                r = pl.ds(i * row_block, row_block)
                normed, rstd = norm(x_ref[0, r, :].astype(f32))
                h1 = (normed * scale + shift).astype(bf16)
                grad = g_qkv[r, :]
                grad_h1 = dot(grad, w_qkv[...], 1, 1)
                w_f32[...] += dot(h1, grad, 0, 0)
                grad_mod[0, 0:1] += row_sum(grad_h1)
                grad_mod[0, 1:2] += row_sum(grad_h1 * normed)
                grad_n = grad_h1 * scale
                out_ref[0, r, :] = (
                    grad_x1[0, r, :]
                    + rstd
                    * (
                        grad_n
                        - jnp.mean(grad_n, -1, keepdims=True)
                        - normed * jnp.mean(grad_n * normed, -1, keepdims=True)
                    )
                ).astype(out_ref.dtype)

        @pl.when(slot < steps)
        def _():
            finish(own_x, own_grad)

        @pl.when(slot >= steps)
        def _():
            finish(far_x, far_grad)

    @pl.when((slot == steps) & (pair == last_pair))
    def _():
        for device in range(2 * chips):
            place = (
                jnp.bitwise_xor(flags[CORE], device & 1) * chips
                + jnp.bitwise_xor(flags[CHIP], device >> 1)
            )
            for part in range(3):
                packed[place, part * rows : (part + 1) * rows] = w_f32[
                    device * rows : (device + 1) * rows, part * width : (part + 1) * width
                ]


def attend_backward(flags, own_x, far_x, qkv, expo, att, grad_att, grad_x1, mod, mine, other):
    steps, length, width = own_x.shape
    slots = steps + 1
    pairs = width // PAIR
    chips = mine.shape[0]
    packed_rows = up_to(3 * width // (2 * chips), 8)

    def const(*zeros):
        return lambda s, p, flags: zeros

    def whole(s, p, flags):
        return (last_live(flags, s, steps), 0, 0)

    def expo_at(s, p, flags):
        at = last_live(flags, s, steps)
        return (at, jnp.where(at == s, p, pairs - 1), 0, 0)

    def block(where):
        return pl.BlockSpec((1, length, width), where)

    def fixed(array_shape):
        return pl.BlockSpec(array_shape, const(*[0] * len(array_shape)))

    spec = pltpu.PrefetchScalarGridSpec(
        num_scalar_prefetch=1,
        grid=(slots, pairs),
        in_specs=[
            block(lambda s, p, flags: (own_slot(flags, s), 0, 0)),
            block(const(0, 0, 0)),
            pl.BlockSpec((1, length, 3 * width), whole),
            pl.BlockSpec((1, 2, length, length), expo_at),
            block(whole), block(whole), block(whole),
            fixed(mod.shape), fixed(mine.shape), fixed(other.shape),
        ],
        out_specs=[
            block(lambda s, p, flags: (jnp.minimum(s, steps - 1), 0, 0)),
            block(const(0, 0, 0)),
            pl.BlockSpec((1, 8, width), lambda s, p, flags: (s, 0, 0)),
            fixed((2 * chips, packed_rows, width)),
        ],
        scratch_shapes=[
            pltpu.VMEM((width, 3 * width), f32),
            pltpu.VMEM((width, 3 * width), bf16),
            pltpu.VMEM((length, 3 * width), bf16),
            pltpu.VMEM((PAIR, length), f32),
            pltpu.VMEM((PAIR, length), f32),
        ],
    )
    shape = jax.ShapeDtypeStruct
    return pl.pallas_call(
        functools.partial(attend_backward_body, steps),
        grid_spec=spec,
        out_shape=[
            shape((steps, length, width), f32),
            shape((1, length, width), bf16),
            shape((slots, 8, width), f32),
            shape((2 * chips, packed_rows, width), f32),
        ],
        compiler_params=pltpu.CompilerParams(vmem_limit_bytes=VMEM_LIMIT),
        cost_estimate=pl.CostEstimate(
            flops=20 * 10**9, bytes_accessed=60 * 10**6, transcendentals=0
        ),
        name="attend_backward",
    )(flags, own_x, far_x, qkv, expo, att, grad_att, grad_x1, mod, mine, other)


def swap(array, mask):
    count = lax.axis_size("dp")
    return lax.ppermute(array, "dp", [(i, i ^ mask) for i in range(count)])


def chip_groups(devices):
    bits = (devices // 2).bit_length() - 1
    if bits == 4:
        return ((2, 3), (1,), (0,))
    return tuple((b,) for b in reversed(range(bits)))


def group_masks(group):
    return [sum(((k >> i) & 1) << b for i, b in enumerate(group)) for k in range(1, 1 << len(group))]


def gather_chips(block):
    held = block[None]
    for group in reversed(chip_groups(lax.axis_size("dp"))):
        held = jnp.concatenate([held] + [swap(held, mask << 1) for mask in group_masks(group)], 0)
    return held


def scatter_core(packed):
    half = packed.shape[0] // 2
    return packed[:half] + swap(packed[half:].astype(bf16), 1).astype(f32)


def scatter_group(held, group):
    masks = group_masks(group)
    part = held.shape[0] // (len(masks) + 1)
    total = held[:part]
    for k, mask in enumerate(masks):
        total = total + swap(held[(k + 1) * part : (k + 2) * part].astype(bf16), mask << 1).astype(f32)
    return total


def body(
    fields, conditions, step_counts, cotangent,
    w_ada, b_ada, w_qkv, w_out, b_out, w_up, b_up, w_down, b_down,
):
    devices = lax.axis_size("dp")
    me = lax.axis_index("dp")
    steps, length, width = fields.shape[1:]
    hidden_units = w_up.shape[1]
    ratio = hidden_units // width
    rows = width // devices
    fields, conditions, cotangent = fields[0], conditions[0], cotangent[0]

    count = step_counts[0]
    head = jnp.concatenate([conditions, jnp.full((4, width), count, bf16)], 0)
    other_head = swap(head, 1)
    other_count = other_head[steps, 0].astype(jnp.int32)
    give = count - other_count >= 2
    take = other_count - count >= 2
    keep = count - give.astype(jnp.int32)
    flags = jnp.stack([keep, take.astype(jnp.int32), me >> 1, me & 1]).astype(jnp.int32)
    far_x = swap(lax.dynamic_index_in_dim(fields, count - 1, 0), 1)
    far_g = swap(lax.dynamic_index_in_dim(cotangent, count - 1, 0), 1)
    far_cond = lax.dynamic_index_in_dim(other_head, other_count - 1, 0)
    cond = jnp.concatenate([conditions, far_cond, jnp.zeros((7 - steps, width), bf16)], 0)
    cond_act = jax.nn.silu(cond.astype(f32)).astype(bf16)

    def columns(shard):
        return [shard[:, i : i + width] for i in range(0, shard.shape[1], width)]

    def whole_bias(shard):
        spread = jnp.where(jnp.arange(devices)[:, None] == me, shard[None, :], jnp.zeros((), bf16))
        return spread.reshape(-1, width)

    biases = [whole_bias(b) for b in (b_ada, b_out, b_up, b_down)]
    first = columns(w_ada) + columns(w_qkv) + biases
    first.append(jnp.zeros((-(9 * rows + 12) % 16, width), bf16))
    second = columns(w_out) + columns(w_up) + [w_down]
    second.append(jnp.zeros((-(1 + 2 * ratio) * rows % 16, width), bf16))
    mine_a = gather_chips(jnp.concatenate(first, 0))
    other_a = swap(mine_a, 1)
    mine_b = gather_chips(jnp.concatenate(second, 0))
    other_b = swap(mine_b, 1)

    qkv, expo, att, inv, mod, bias = attend_forward(
        flags, fields, far_x, cond_act, mine_a, other_a
    )
    own_out, far_out, grad_x1, grad_att, grad_mod2, packed2, bias_sum = feed_forward(
        flags, fields, far_x, cotangent, far_g, att, inv, mod, bias, mine_b, other_b, hidden_units
    )
    groups = chip_groups(devices)
    held2 = scatter_core(packed2)
    for group in groups:
        held2 = scatter_group(held2, group)
    own_grad, far_grad, grad_mod1, packed1 = attend_backward(
        flags, fields, far_x, qkv, expo, att, grad_att, grad_x1, mod, mine_a, other_a
    )
    held1 = scatter_core(packed1)
    for group in groups:
        held1 = scatter_group(held1, group)
    sums1, sums2 = held1[0], held2[0]

    grad_mod = (grad_mod1 + grad_mod2)[:, :6].reshape(-1, width)
    note = jnp.concatenate([grad_mod, bias_sum.reshape(-1, width), cond_act.astype(f32)], 0)
    note = note.astype(bf16)
    slots = steps + 1
    note = jnp.concatenate([note, jnp.zeros((-note.shape[0] % 16, width), bf16)], 0)
    mine_n = gather_chips(note)
    notes = jnp.concatenate([mine_n, swap(mine_n, 1)], 0)
    all_mod = notes[:, : 6 * slots].reshape(devices * slots, 6 * width)
    all_bias = jnp.sum(notes[:, 6 * slots : 6 * slots + 6].astype(f32), 0).reshape(-1)
    all_cond = notes[:, 6 * slots + 6 : 7 * slots + 6].reshape(devices * slots, width)
    own_cond = lax.dynamic_slice_in_dim(all_cond, me * rows, rows, 1)
    grad_ada = jnp.einsum("sm,sn->mn", own_cond, all_mod, preferred_element_type=f32)
    sum_ada = jnp.sum(all_mod.astype(f32), 0)

    def own_part(vector):
        size = vector.shape[0] // devices
        return lax.dynamic_slice_in_dim(vector, me * size, size, 0)

    back_out = swap(far_out, 1)
    back_grad = swap(far_grad, 1).astype(f32)

    def put_back(array, back):
        now = lax.dynamic_index_in_dim(array, count - 1, 0)
        return lax.dynamic_update_index_in_dim(array, jnp.where(give, back, now), count - 1, 0)

    def from_columns(block, start, parts):
        return jnp.concatenate(
            [block[start + i * rows : start + (i + 1) * rows] for i in range(parts)], 1
        )

    return (
        put_back(own_out, back_out)[None],
        put_back(own_grad, back_grad)[None],
        grad_ada,
        own_part(sum_ada),
        from_columns(sums1, 0, 3),
        sums2[:rows],
        own_part(all_bias[:width]),
        from_columns(sums2, rows, ratio),
        own_part(all_bias[width : width + hidden_units]),
        sums2[(1 + ratio) * rows : (1 + 2 * ratio) * rows],
        own_part(all_bias[width + hidden_units :]),
    )


def solution(mesh):
    item, matrix, vector = P("dp", None, None, None), P("dp", None), P("dp")
    return jax.shard_map(
        body,
        mesh=mesh,
        in_specs=(
            item, P("dp", None, None), vector, item,
            matrix, vector, matrix, matrix, vector, matrix, vector, matrix, vector,
        ),
        out_specs=(
            item, item, matrix, vector, matrix, matrix, vector, matrix, vector, matrix, vector,
        ),
        check_vma=False,
    )
```

time: 1380 us -> 358 us (0.26); the launches traced: 1360 us -> 355 us
  matrix products: 511 us -> 1.88 us
  blocking collectives: 263 us -> 0 us
  other arithmetic: 249 us -> 12.2 us
  local copies, waits for them, and re-layouts: 175 us -> 37 us
  Pallas kernels: 0 us -> 78 us
  waiting for transfers between devices: 28.3 us -> 96.5 us
  starting transfers between devices: 83.7 us -> 127 us
  loops' own time: 35.7 us -> 0 us
    dot_general x210 -> x1, matrix products: 511 us -> 1.88 us  [body(): jnp.einsum('sm,sn->mn', own_cond, all_mod, preferred_element_type=f32)]
    unnamed x3 -> x0, blocking collectives: 179 us -> none
    reduce_sum x81 -> x2, other arithmetic: 130 us -> 0.2 us  [the longest x1 0.12 us: body(): sum_ada = jnp.sum(all_mod.astype(f32), 0)]
    ppermute x37 -> x35, starting transfers between devices: 15.7 us -> 127 us  [swap(): return lax.ppermute(array, 'dp', [(i, i ^ mask) for i in range(count)])]
    ppermute x37 -> x35, waiting for transfers between devices: 0.1 us -> 96.5 us  [swap(): return lax.ppermute(array, 'dp', [(i, i ^ mask) for i in range(count)])]
    all_gather x2 -> x0, blocking collectives: 84.8 us -> none  [the longest x1 47 us: body(): lax.all_gather(w_qkv, 'dp', axis=0, tiled=True)]
    pallas_call x0 -> x3, Pallas kernels: none -> 78 us  [the longest x1 29.6 us: attend_backward(): pl.pallas_call(functools.partial(attend_backward_body, steps), grid_spec=...]
    unnamed x25 -> x0, starting transfers between devices: 67.9 us -> none
  transfers between devices with their start and end apart: 66 -> 35, of which waited for: 3 -> 16; matrix products, arithmetic and copies ran while one was open for 23% -> 10% of each run, Pallas kernels for 0% -> 6%
where the time goes in v1:
time: 358 us; the launch traced here: 355 us
  starting transfers between devices  127 us (35%)
  waiting for transfers between devices  96.5 us (27%)
  Pallas kernels  78 us (22%)
  local copies, waits for them, and re-layouts  37 us (10%)
  other arithmetic  12.2 us (3%)
    ppermute x35, starting transfers between devices, swap(): return lax.ppermute(array, 'dp', [(i, i ^ mask) for i in range(count)])  127 us
    ppermute x35, waiting for transfers between devices, swap(): return lax.ppermute(array, 'dp', [(i, i ^ mask) for i in range(count)])  96.5 us
    pallas_call x1, Pallas kernels, attend_backward(): pl.pallas_call(functools.partial(attend_backward_body, steps), grid_spec=...  29.6 us
    pallas_call x1, Pallas kernels, feed_forward(): pl.pallas_call(functools.partial(feed_forward_body, steps), grid_spec=spe...  26.7 us
    pallas_call x1, Pallas kernels, attend_forward(): pl.pallas_call(functools.partial(attend_forward_body, steps), grid_spec=s...  21.7 us
    unnamed x46, local copies, waits for them, and re-layouts  12.5 us
  transfers between devices with their start and end apart: 35, of which 16 were waited for; matrix products, arithmetic and copies ran while one was open for 10% of the time, Pallas kernels for 6%

profile of v1, /device:TPU:0, one launch (start us, length us, event | category | flops | bytes accessed | tf_op | source)
XLA Modules:
  0.0 354.8 jit_solution(4596444853693254578)
XLA Ops:
  5.1 3.0 collective-permute-start.3
  10.9 2.0 collective-permute-start.4
  12.9 2.3 collective-permute-done.9
  18.2 2.1 collective-permute-start.5
  20.3 2.7 collective-permute-start.6
  24.7 13.0 %collective-permute-done.5 = bf16[4,128,384]{2,1,0:T(8,128)(2,1)S(1)} collective-permute-done((bf16[4,128,384]{2,1,0:T(8,128)(2,1)S(1)}, bf16[4,128,384]{2,1,0:T(8,128)(2,1)S(1)}, u32[]{:S(2)}, u32[]{:S(2)}) %collective-permute-start.5) | collective-permute-done | bytes 393248 | tf_op jit(solution)/shard_map/ppermute | solution.py:588
  37.8 12.4 %collective-permute-done.6 = bf16[4,128,384]{2,1,0:T(8,128)(2,1)S(1)} collective-permute-done((bf16[4,128,384]{2,1,0:T(8,128)(2,1)S(1)}, bf16[4,128,384]{2,1,0:T(8,128)(2,1)S(1)}, u32[]{:S(2)}, u32[]{:S(2)}) %collective-permute-start.6) | collective-permute-done | bytes 393248 | tf_op jit(solution)/shard_map/ppermute | solution.py:588
  51.9 6.0 %collective-permute-start.12 = (bf16[4,112,384]{2,1,0:T(8,128)(2,1)}, bf16[4,112,384]{2,1,0:T(8,128)(2,1)S(1)}, u32[]{:S(2)}, u32[]{:S(2)}) collective-permute-start(bf16[4,112,384]{2,1,0:T(8,128)(2,1)} %pad_maximum_fusion.1), channel_id=1, source_target_pairs={{0,16},{1,17},{2,18},{3,19},{4,20},{5,21},{6,22},{7,23},{8,24},{9,... | collective-permute-start | bytes 1032200 | tf_op jit(solution)/shard_map/ppermute | solution.py:588
  62.3 19.4 %collective-permute-done.12 = bf16[4,112,384]{2,1,0:T(8,128)(2,1)S(1)} collective-permute-done((bf16[4,112,384]{2,1,0:T(8,128)(2,1)}, bf16[4,112,384]{2,1,0:T(8,128)(2,1)S(1)}, u32[]{:S(2)}, u32[]{:S(2)}) %collective-permute-start.12) | collective-permute-done | bytes 344096 | tf_op jit(solution)/shard_map/ppermute | solution.py:588
  83.3 2.1 dynamic-slice_bitcast_fusion.1
  85.9 2.1 dynamic-slice_bitcast_fusion
  92.3 21.7 %attend_forward.1 = (bf16[5,1024,1152]{2,1,0:T(8,128)(2,1)}, bf16[5,6,1024,1024]{3,2,1,0:T(8,128)(2,1)}, bf16[5,1024,384]{2,1,0:T(8,128)(2,1)}, f32[5,1024,384]{...) custom-call(s32[4]{0:T(128)} %pad_add_fusion.flags, bf16[4,1024,384]{2,1,0:T(8,128)(2,1)} %bitcast.60, ...), custom_call_target="tpu_custom_call" | custom-call | flops 6000000000 | bytes 40000000 | tf_op jit(solution)/shard_map/attend_forward/pallas_call | solution.py:186
  114.0 26.7 %feed_forward.1 = (bf16[4,1024,384]{2,1,0:T(8,128)(2,1)}, bf16[1,1024,384]{2,1,0:T(8,128)(2,1)}, f32[5,1024,384]{2,1,0:T(8,128)}, bf16[5,1024,384]{2,1,0:T(8,128...) custom-call(s32[4]{0:T(128)} %pad_add_fusion.flags, bf16[4,1024,384]{2,1,0:T(8,128)(2,1)} %bitcast.61, ...), custom_call_target="tpu_custom_call" | custom-call | flops 20000000000 | bytes 40000000 | tf_op jit(solution)/shard_map/feed_forward/pallas_call | solution.py:381
  140.7 29.6 %attend_backward.1 = (f32[4,1024,384]{2,1,0:T(8,128)}, bf16[1,1024,384]{2,1,0:T(8,128)(2,1)}, f32[5,8,384]{2,1,0:T(8,128)}, f32[32,40,384]{2,1,0:T(8,128)}) custom-call(s32[4]{0:T(128)} %pad_add_fusion.flags, bf16[4,1024,384]{2,1,0:T(8,128)(2,1)} %bitcast.62, bf16[1,1024,384]{2,1,0:T(8,128)(2,1)} %collective-permute-done.1.far_x, ...), custom_call_target="tpu_custom_call" | custom-call | flops 20000000000 | bytes 60000000 | tf_op jit(solution)/shard_map/attend_backward/pallas_call | solution.py:569
  172.7 84.9 %collective-permute-start.17 = (bf16[1,48,384]{2,1,0:T(8,128)(2,1)S(1)}, bf16[1,48,384]{2,1,0:T(8,128)(2,1)S(1)}, u32[]{:S(2)}, u32[]{:S(2)}) collective-permute-start(bf16[1,48,384]{2,1,0:T(8,128)(2,1)S(1)} %fusion.12), channel_id=1, source_target_pairs={{0,2},{1,3},{2,0},{3,1},{4,6},{5,7},{6,4},{7,5},{8,10},{9,11},{10,... | collective-permute-start | bytes 110600 | tf_op jit(solution)/shard_map/ppermute | solution.py:588
  257.6 1.9 slice.327
  259.8 2.9 copy.35
  263.9 4.4 %collective-permute-done.18 = bf16[2,48,384]{2,1,0:T(8,128)(2,1)S(1)} collective-permute-done((bf16[2,48,384]{2,1,0:T(8,128)(2,1)S(1)}, bf16[2,48,384]{2,1,0:T(8,128)(2,1)S(1)}, u32[]{:S(2)}, u32[]{:S(2)}) %collective-permute-start.18) | collective-permute-done | bytes 73760 | tf_op jit(solution)/shard_map/ppermute | solution.py:588
  270.7 6.8 %collective-permute-start.25 = (bf16[4,40,384]{2,1,0:T(8,128)(2,1)S(1)}, bf16[4,40,384]{2,1,0:T(8,128)(2,1)S(1)}, u32[]{:S(2)}, u32[]{:S(2)}) collective-permute-start(bf16[4,40,384]{2,1,0:T(8,128)(2,1)S(1)} %get-tuple-element.54), channel_id=1, source_target_pairs={{0,16},{1,17},{2,18},{3,19},{4,20},{5,21},{6,22},{7,23},{8,24},{9,... | collective-permute-start | bytes 368648 | tf_op jit(solution)/shard_map/ppermute | solution.py:588
  278.3 3.2 collective-permute-done.25
  281.5 4.0 %collective-permute-start.20 = (bf16[4,48,384]{2,1,0:T(8,128)(2,1)S(1)}, bf16[4,48,384]{2,1,0:T(8,128)(2,1)S(1)}, u32[]{:S(2)}, u32[]{:S(2)}) collective-permute-start(bf16[4,48,384]{2,1,0:T(8,128)(2,1)S(1)} %pad_maximum_fusion.4), channel_id=1, source_target_pairs={{0,16},{1,17},{2,18},{3,19},{4,20},{5,21},{6,22},{7,23},{8,24},{9,... | collective-permute-start | bytes 442376 | tf_op jit(solution)/shard_map/ppermute | solution.py:588
  285.5 2.6 collective-permute-done.26
  289.7 7.8 %collective-permute-done.20 = bf16[4,48,384]{2,1,0:T(8,128)(2,1)S(1)} collective-permute-done((bf16[4,48,384]{2,1,0:T(8,128)(2,1)S(1)}, bf16[4,48,384]{2,1,0:T(8,128)(2,1)S(1)}, u32[]{:S(2)}, u32[]{:S(2)}) %collective-permute-start.20) | collective-permute-done | bytes 147488 | tf_op jit(solution)/shard_map/ppermute | solution.py:588
  298.1 3.7 %collective-permute-done.27 = bf16[2,40,384]{2,1,0:T(8,128)(2,1)S(1)} collective-permute-done((bf16[2,40,384]{2,1,0:T(8,128)(2,1)S(1)}, bf16[2,40,384]{2,1,0:T(8,128)(2,1)S(1)}, u32[]{:S(2)}, u32[]{:S(2)}) %collective-permute-start.27) | collective-permute-done | bytes 61472 | tf_op jit(solution)/shard_map/ppermute | solution.py:588
  302.0 3.7 %collective-permute-done.28 = bf16[1,40,384]{2,1,0:T(8,128)(2,1)S(1)} collective-permute-done((bf16[1,40,384]{2,1,0:T(8,128)(2,1)S(1)}, bf16[1,40,384]{2,1,0:T(8,128)(2,1)S(1)}, u32[]{:S(2)}, u32[]{:S(2)}) %collective-permute-start.28) | collective-permute-done | bytes 30752 | tf_op jit(solution)/shard_map/ppermute | solution.py:588
  306.7 2.8 bitcast_dynamic-update-slice_fusion
  310.2 2.1 copy-done
  313.2 3.1 collective-permute-start.31
  324.7 2.6 collective-permute-done.30
  327.4 13.1 %collective-permute-done.31 = bf16[4,112,384]{2,1,0:T(8,128)(2,1)} collective-permute-done((bf16[4,112,384]{2,1,0:T(8,128)(2,1)}, bf16[4,112,384]{2,1,0:T(8,128)(2,1)}, u32[]{:S(2)}, u32[]{:S(2)}) %collective-permute-start.31) | collective-permute-done | bytes 344096 | tf_op jit(solution)/shard_map/ppermute | solution.py:588
  344.4 2.9 collective-permute-done.33
  349.0 3.9 %collective-permute-done.34 = bf16[1,112,384]{2,1,0:T(8,128)(2,1)S(1)} collective-permute-done((bf16[1,112,384]{2,1,0:T(8,128)(2,1)S(1)}, bf16[1,112,384]{2,1,0:T(8,128)(2,1)S(1)}, u32[]{:S(2)}, u32[]{:S(2)}) %collective-permute-start.34) | collective-permute-done | bytes 86048 | tf_op jit(solution)/shard_map/ppermute | solution.py:588
  (168 shorter events, 50.6 us)
Async XLA Ops:
  5.1 5.8 %collective-permute-start.3 = (bf16[1,128,384]{2,1,0:T(8,128)(2,1)S(1)}, bf16[1,128,384]{2,1,0:T(8,128)(2,1)S(1)}, u32[]{:S(2)}, u32[]{:S(2)}) collective-permute-start(bf16[1,128,384]{2,1,0:T(8,128)(2,1)S(1)} %bitcast.66), channel_id=1, source_target_pairs={{0,2},{1,3},{2,0},{3,1},{4,6},{5,7},{6,4},{7,5},{8,10},{9,11},{10,... | collective-permute-start | bytes 294920 | tf_op jit(solution)/shard_map/ppermute | solution.py:588
  10.7 4.5 %collective-permute-start.9 = (bf16[1,112,384]{2,1,0:T(8,128)(2,1)S(1)}, bf16[1,112,384]{2,1,0:T(8,128)(2,1)S(1)}, u32[]{:S(2)}, u32[]{:S(2)}) collective-permute-start(bf16[1,112,384]{2,1,0:T(8,128)(2,1)S(1)} %bitcast.69), channel_id=1, source_target_pairs={{0,2},{1,3},{2,0},{3,1},{4,6},{5,7},{6,4},{7,5},{8,10},{9,11},{10,... | collective-permute-start | bytes 258056 | tf_op jit(solution)/shard_map/ppermute | solution.py:588
  10.9 7.2 %collective-permute-start.4 = (bf16[2,128,384]{2,1,0:T(8,128)(2,1)S(1)}, bf16[2,128,384]{2,1,0:T(8,128)(2,1)S(1)}, u32[]{:S(2)}, u32[]{:S(2)}) collective-permute-start(bf16[2,128,384]{2,1,0:T(8,128)(2,1)S(1)} %pad_maximum_fusion.2), channel_id=1, source_target_pairs={{0,4},{1,5},{2,6},{3,7},{4,0},{5,1},{6,2},{7,3},{8,12},{9,13},{10,... | collective-permute-start | bytes 589832 | tf_op jit(solution)/shard_map/ppermute | solution.py:588
  15.3 7.8 %collective-permute-start.10 = (bf16[2,112,384]{2,1,0:T(8,128)(2,1)S(1)}, bf16[2,112,384]{2,1,0:T(8,128)(2,1)S(1)}, u32[]{:S(2)}, u32[]{:S(2)}) collective-permute-start(bf16[2,112,384]{2,1,0:T(8,128)(2,1)S(1)} %pad_maximum_fusion.3), channel_id=1, source_target_pairs={{0,4},{1,5},{2,6},{3,7},{4,0},{5,1},{6,2},{7,3},{8,12},{9,13},{10,... | collective-permute-start | bytes 516104 | tf_op jit(solution)/shard_map/ppermute | solution.py:588
  18.2 19.5 %collective-permute-start.5 = (bf16[4,128,384]{2,1,0:T(8,128)(2,1)S(1)}, bf16[4,128,384]{2,1,0:T(8,128)(2,1)S(1)}, u32[]{:S(2)}, u32[]{:S(2)}) collective-permute-start(bf16[4,128,384]{2,1,0:T(8,128)(2,1)S(1)} %pad_maximum_fusion), channel_id=1, source_target_pairs={{0,8},{1,9},{2,10},{3,11},{4,12},{5,13},{6,14},{7,15},{8,0},{9,1},... | collective-permute-start | bytes 1179656 | tf_op jit(solution)/shard_map/ppermute | solution.py:588
  20.3 29.9 %collective-permute-start.6 = (bf16[4,128,384]{2,1,0:T(8,128)(2,1)S(1)}, bf16[4,128,384]{2,1,0:T(8,128)(2,1)S(1)}, u32[]{:S(2)}, u32[]{:S(2)}) collective-permute-start(bf16[4,128,384]{2,1,0:T(8,128)(2,1)S(1)} %pad_maximum_fusion), channel_id=1, source_target_pairs={{0,16},{1,17},{2,18},{3,19},{4,20},{5,21},{6,22},{7,23},{8,24},{9,... | collective-permute-start | bytes 1179656 | tf_op jit(solution)/shard_map/ppermute | solution.py:588
  23.0 27.3 %collective-permute-start.7 = (bf16[4,128,384]{2,1,0:T(8,128)(2,1)S(1)}, bf16[4,128,384]{2,1,0:T(8,128)(2,1)S(1)}, u32[]{:S(2)}, u32[]{:S(2)}) collective-permute-start(bf16[4,128,384]{2,1,0:T(8,128)(2,1)S(1)} %pad_maximum_fusion), channel_id=1, source_target_pairs={{0,24},{1,25},{2,26},{3,27},{4,28},{5,29},{6,30},{7,31},{8,16},{9,... | collective-permute-start | bytes 1179656 | tf_op jit(solution)/shard_map/ppermute | solution.py:588
  23.8 36.7 %collective-permute-start.11 = (bf16[4,112,384]{2,1,0:T(8,128)(2,1)}, bf16[4,112,384]{2,1,0:T(8,128)(2,1)}, u32[]{:S(2)}, u32[]{:S(2)}) collective-permute-start(bf16[4,112,384]{2,1,0:T(8,128)(2,1)} %pad_maximum_fusion.1), channel_id=1, source_target_pairs={{0,8},{1,9},{2,10},{3,11},{4,12},{5,13},{6,14},{7,15},{8,0},{9,1},... | collective-permute-start | bytes 1032200 | tf_op jit(solution)/shard_map/ppermute | solution.py:588
  50.4 40.8 %collective-permute-start.8 = (bf16[16,128,384]{2,1,0:T(8,128)(2,1)S(1)}, bf16[16,128,384]{2,1,0:T(8,128)(2,1)S(1)}, u32[]{:S(2)}, u32[]{:S(2)}) collective-permute-start(bf16[16,128,384]{2,1,0:T(8,128)(2,1)S(1)} %constant_dynamic-update-slice_fusion.mine), channel_id=1, source_target_pairs={{0,1},{1,0},{2,3},{3,2},{4,5},{5,4},{6,7},{7,6},{8,9},{9,8},{10,11... | collective-permute-start | bytes 4718600 | tf_op jit(solution)/shard_map/ppermute | solution.py:588
  51.9 29.9 %collective-permute-start.12 = (bf16[4,112,384]{2,1,0:T(8,128)(2,1)}, bf16[4,112,384]{2,1,0:T(8,128)(2,1)S(1)}, u32[]{:S(2)}, u32[]{:S(2)}) collective-permute-start(bf16[4,112,384]{2,1,0:T(8,128)(2,1)} %pad_maximum_fusion.1), channel_id=1, source_target_pairs={{0,16},{1,17},{2,18},{3,19},{4,20},{5,21},{6,22},{7,23},{8,24},{9,... | collective-permute-start | bytes 1032200 | tf_op jit(solution)/shard_map/ppermute | solution.py:588
  58.5 24.0 %collective-permute-start.13 = (bf16[4,112,384]{2,1,0:T(8,128)(2,1)}, bf16[4,112,384]{2,1,0:T(8,128)(2,1)S(1)}, u32[]{:S(2)}, u32[]{:S(2)}) collective-permute-start(bf16[4,112,384]{2,1,0:T(8,128)(2,1)} %pad_maximum_fusion.1), channel_id=1, source_target_pairs={{0,24},{1,25},{2,26},{3,27},{4,28},{5,29},{6,30},{7,31},{8,16},{9,... | collective-permute-start | bytes 1032200 | tf_op jit(solution)/shard_map/ppermute | solution.py:588
  83.3 30.8 %collective-permute-start.14 = (bf16[16,112,384]{2,1,0:T(8,128)(2,1)}, bf16[16,112,384]{2,1,0:T(8,128)(2,1)}, u32[]{:S(2)}, u32[]{:S(2)}) collective-permute-start(bf16[16,112,384]{2,1,0:T(8,128)(2,1)} %constant_dynamic-update-slice_fusion.6.mine), channel_id=1, source_target_pairs={{0,1},{1,0},{2,3},{3,2},{4,5},{5,4},{6,7},{7,6},{8,9},{9,8},{10,11... | collective-permute-start | bytes 4128776 | tf_op jit(solution)/shard_map/ppermute | solution.py:588
  85.3 5.8 %collective-permute-start.1 = (bf16[1,1024,384]{2,1,0:T(8,128)(2,1)}, bf16[1,1024,384]{2,1,0:T(8,128)(2,1)}, u32[]{:S(2)}, u32[]{:S(2)}) collective-permute-start(bf16[1,1024,384]{2,1,0:T(8,128)(2,1)} %dynamic-slice_bitcast_fusion.1), channel_id=1, source_target_pairs={{0,1},{1,0},{2,3},{3,2},{4,5},{5,4},{6,7},{7,6},{8,9},{9,8},{10,11... | collective-permute-start | bytes 2359304 | tf_op jit(solution)/shard_map/ppermute | solution.py:588
  88.1 25.9 %collective-permute-start.2 = (bf16[1,1024,384]{2,1,0:T(8,128)(2,1)}, bf16[1,1024,384]{2,1,0:T(8,128)(2,1)}, u32[]{:S(2)}, u32[]{:S(2)}) collective-permute-start(bf16[1,1024,384]{2,1,0:T(8,128)(2,1)} %dynamic-slice_bitcast_fusion), channel_id=1, source_target_pairs={{0,1},{1,0},{2,3},{3,2},{4,5},{5,4},{6,7},{7,6},{8,9},{9,8},{10,11... | collective-permute-start | bytes 2359304 | tf_op jit(solution)/shard_map/ppermute | solution.py:588
  171.6 97.0 %collective-permute-start.23 = (bf16[16,40,384]{2,1,0:T(8,128)(2,1)S(1)}, bf16[16,40,384]{2,1,0:T(8,128)(2,1)S(1)}, u32[]{:S(2)}, u32[]{:S(2)}) collective-permute-start(bf16[16,40,384]{2,1,0:T(8,128)(2,1)S(1)} %slice.328), channel_id=1, source_target_pairs={{0,1},{1,0},{2,3},{3,2},{4,5},{5,4},{6,7},{7,6},{8,9},{9,8},{10,11... | collective-permute-start | bytes 1474568 | tf_op jit(solution)/shard_map/ppermute | solution.py:588
  172.7 91.1 %collective-permute-start.17 = (bf16[1,48,384]{2,1,0:T(8,128)(2,1)S(1)}, bf16[1,48,384]{2,1,0:T(8,128)(2,1)S(1)}, u32[]{:S(2)}, u32[]{:S(2)}) collective-permute-start(bf16[1,48,384]{2,1,0:T(8,128)(2,1)S(1)} %fusion.12), channel_id=1, source_target_pairs={{0,2},{1,3},{2,0},{3,1},{4,6},{5,7},{6,4},{7,5},{8,10},{9,11},{10,... | collective-permute-start | bytes 110600 | tf_op jit(solution)/shard_map/ppermute | solution.py:588
  259.5 50.2 %collective-permute-start.29 = (bf16[16,112,384]{2,1,0:T(8,128)(2,1)S(1)}, bf16[16,112,384]{2,1,0:T(8,128)(2,1)S(1)}, u32[]{:S(2)}, u32[]{:S(2)}) collective-permute-start(bf16[16,112,384]{2,1,0:T(8,128)(2,1)S(1)} %slice.327), channel_id=1, source_target_pairs={{0,1},{1,0},{2,3},{3,2},{4,5},{5,4},{6,7},{7,6},{8,9},{9,8},{10,11... | collective-permute-start | bytes 4128776 | tf_op jit(solution)/shard_map/ppermute | solution.py:588
  263.8 4.5 %collective-permute-start.18 = (bf16[2,48,384]{2,1,0:T(8,128)(2,1)S(1)}, bf16[2,48,384]{2,1,0:T(8,128)(2,1)S(1)}, u32[]{:S(2)}, u32[]{:S(2)}) collective-permute-start(bf16[2,48,384]{2,1,0:T(8,128)(2,1)S(1)} %pad_maximum_fusion.6), channel_id=1, source_target_pairs={{0,4},{1,5},{2,6},{3,7},{4,0},{5,1},{6,2},{7,3},{8,12},{9,13},{10,... | collective-permute-start | bytes 221192 | tf_op jit(solution)/shard_map/ppermute | solution.py:588
  268.4 9.1 %collective-permute-start.19 = (bf16[4,48,384]{2,1,0:T(8,128)(2,1)S(1)}, bf16[4,48,384]{2,1,0:T(8,128)(2,1)S(1)}, u32[]{:S(2)}, u32[]{:S(2)}) collective-permute-start(bf16[4,48,384]{2,1,0:T(8,128)(2,1)S(1)} %pad_maximum_fusion.4), channel_id=1, source_target_pairs={{0,8},{1,9},{2,10},{3,11},{4,12},{5,13},{6,14},{7,15},{8,0},{9,1},... | collective-permute-start | bytes 442376 | tf_op jit(solution)/shard_map/ppermute | solution.py:588
  268.8 8.9 %collective-permute-start.24 = (bf16[4,40,384]{2,1,0:T(8,128)(2,1)S(1)}, bf16[4,40,384]{2,1,0:T(8,128)(2,1)S(1)}, u32[]{:S(2)}, u32[]{:S(2)}) collective-permute-start(bf16[4,40,384]{2,1,0:T(8,128)(2,1)S(1)} %get-tuple-element.52), channel_id=1, source_target_pairs={{0,8},{1,9},{2,10},{3,11},{4,12},{5,13},{6,14},{7,15},{8,0},{9,1},... | collective-permute-start | bytes 368648 | tf_op jit(solution)/shard_map/ppermute | solution.py:588
  270.7 10.7 %collective-permute-start.25 = (bf16[4,40,384]{2,1,0:T(8,128)(2,1)S(1)}, bf16[4,40,384]{2,1,0:T(8,128)(2,1)S(1)}, u32[]{:S(2)}, u32[]{:S(2)}) collective-permute-start(bf16[4,40,384]{2,1,0:T(8,128)(2,1)S(1)} %get-tuple-element.54), channel_id=1, source_target_pairs={{0,16},{1,17},{2,18},{3,19},{4,20},{5,21},{6,22},{7,23},{8,24},{9,... | collective-permute-start | bytes 368648 | tf_op jit(solution)/shard_map/ppermute | solution.py:588
  277.5 10.6 %collective-permute-start.26 = (bf16[4,40,384]{2,1,0:T(8,128)(2,1)S(1)}, bf16[4,40,384]{2,1,0:T(8,128)(2,1)S(1)}, u32[]{:S(2)}, u32[]{:S(2)}) collective-permute-start(bf16[4,40,384]{2,1,0:T(8,128)(2,1)S(1)} %get-tuple-element.53), channel_id=1, source_target_pairs={{0,24},{1,25},{2,26},{3,27},{4,28},{5,29},{6,30},{7,31},{8,16},{9,... | collective-permute-start | bytes 368648 | tf_op jit(solution)/shard_map/ppermute | solution.py:588
  277.6 29.1 %collective-permute-start.16 = (bf16[1,1024,384]{2,1,0:T(8,128)(2,1)S(1)}, bf16[1,1024,384]{2,1,0:T(8,128)(2,1)S(1)}, u32[]{:S(2)}, u32[]{:S(2)}) collective-permute-start(bf16[1,1024,384]{2,1,0:T(8,128)(2,1)S(1)} %copy-done.12), channel_id=1, source_target_pairs={{0,1},{1,0},{2,3},{3,2},{4,5},{5,4},{6,7},{7,6},{8,9},{9,8},{10,11... | collective-permute-start | bytes 2359304 | tf_op jit(solution)/shard_map/ppermute | solution.py:588
  277.7 28.7 %collective-permute-start.15 = (bf16[1,1024,384]{2,1,0:T(8,128)(2,1)S(1)}, bf16[1,1024,384]{2,1,0:T(8,128)(2,1)S(1)}, u32[]{:S(2)}, u32[]{:S(2)}) collective-permute-start(bf16[1,1024,384]{2,1,0:T(8,128)(2,1)S(1)} %copy-done.11), channel_id=1, source_target_pairs={{0,1},{1,0},{2,3},{3,2},{4,5},{5,4},{6,7},{7,6},{8,9},{9,8},{10,11... | collective-permute-start | bytes 2359304 | tf_op jit(solution)/shard_map/ppermute | solution.py:588
  281.5 16.1 %collective-permute-start.20 = (bf16[4,48,384]{2,1,0:T(8,128)(2,1)S(1)}, bf16[4,48,384]{2,1,0:T(8,128)(2,1)S(1)}, u32[]{:S(2)}, u32[]{:S(2)}) collective-permute-start(bf16[4,48,384]{2,1,0:T(8,128)(2,1)S(1)} %pad_maximum_fusion.4), channel_id=1, source_target_pairs={{0,16},{1,17},{2,18},{3,19},{4,20},{5,21},{6,22},{7,23},{8,24},{9,... | collective-permute-start | bytes 442376 | tf_op jit(solution)/shard_map/ppermute | solution.py:588
  288.1 13.7 %collective-permute-start.21 = (bf16[4,48,384]{2,1,0:T(8,128)(2,1)S(1)}, bf16[4,48,384]{2,1,0:T(8,128)(2,1)S(1)}, u32[]{:S(2)}, u32[]{:S(2)}) collective-permute-start(bf16[4,48,384]{2,1,0:T(8,128)(2,1)S(1)} %pad_maximum_fusion.4), channel_id=1, source_target_pairs={{0,24},{1,25},{2,26},{3,27},{4,28},{5,29},{6,30},{7,31},{8,16},{9,... | collective-permute-start | bytes 442376 | tf_op jit(solution)/shard_map/ppermute | solution.py:588
  301.9 7.6 %collective-permute-start.22 = (bf16[16,48,384]{2,1,0:T(8,128)(2,1)S(1)}, bf16[16,48,384]{2,1,0:T(8,128)(2,1)S(1)}, u32[]{:S(2)}, u32[]{:S(2)}) collective-permute-start(bf16[16,48,384]{2,1,0:T(8,128)(2,1)S(1)} %get-tuple-element.60), channel_id=1, source_target_pairs={{0,1},{1,0},{2,3},{3,2},{4,5},{5,4},{6,7},{7,6},{8,9},{9,8},{10,11... | collective-permute-start | bytes 1769480 | tf_op jit(solution)/shard_map/ppermute | solution.py:588
  313.2 14.1 %collective-permute-start.30 = (bf16[4,112,384]{2,1,0:T(8,128)(2,1)}, bf16[4,112,384]{2,1,0:T(8,128)(2,1)}, u32[]{:S(2)}, u32[]{:S(2)}) collective-permute-start(bf16[4,112,384]{2,1,0:T(8,128)(2,1)} %get-tuple-element.49), channel_id=1, source_target_pairs={{0,8},{1,9},{2,10},{3,11},{4,12},{5,13},{6,14},{7,15},{8,0},{9,1},... | collective-permute-start | bytes 1032200 | tf_op jit(solution)/shard_map/ppermute | solution.py:588
  313.2 27.2 %collective-permute-start.31 = (bf16[4,112,384]{2,1,0:T(8,128)(2,1)}, bf16[4,112,384]{2,1,0:T(8,128)(2,1)}, u32[]{:S(2)}, u32[]{:S(2)}) collective-permute-start(bf16[4,112,384]{2,1,0:T(8,128)(2,1)} %get-tuple-element.51), channel_id=1, source_target_pairs={{0,16},{1,17},{2,18},{3,19},{4,20},{5,21},{6,22},{7,23},{8,24},{9,... | collective-permute-start | bytes 1032200 | tf_op jit(solution)/shard_map/ppermute | solution.py:588
  316.4 24.0 %collective-permute-start.32 = (bf16[4,112,384]{2,1,0:T(8,128)(2,1)}, bf16[4,112,384]{2,1,0:T(8,128)(2,1)}, u32[]{:S(2)}, u32[]{:S(2)}) collective-permute-start(bf16[4,112,384]{2,1,0:T(8,128)(2,1)} %get-tuple-element.50), channel_id=1, source_target_pairs={{0,24},{1,25},{2,26},{3,27},{4,28},{5,29},{6,30},{7,31},{8,16},{9,... | collective-permute-start | bytes 1032200 | tf_op jit(solution)/shard_map/ppermute | solution.py:588
  341.8 5.5 %collective-permute-start.33 = (bf16[2,112,384]{2,1,0:T(8,128)(2,1)S(1)}, bf16[2,112,384]{2,1,0:T(8,128)(2,1)S(1)}, u32[]{:S(2)}, u32[]{:S(2)}) collective-permute-start(bf16[2,112,384]{2,1,0:T(8,128)(2,1)S(1)} %slice.329), channel_id=1, source_target_pairs={{0,4},{1,5},{2,6},{3,7},{4,0},{5,1},{6,2},{7,3},{8,12},{9,13},{10,... | collective-permute-start | bytes 516104 | tf_op jit(solution)/shard_map/ppermute | solution.py:588
  348.3 4.6 %collective-permute-start.34 = (bf16[1,112,384]{2,1,0:T(8,128)(2,1)S(1)}, bf16[1,112,384]{2,1,0:T(8,128)(2,1)S(1)}, u32[]{:S(2)}, u32[]{:S(2)}) collective-permute-start(bf16[1,112,384]{2,1,0:T(8,128)(2,1)S(1)} %slice.330), channel_id=1, source_target_pairs={{0,2},{1,3},{2,0},{3,1},{4,6},{5,7},{6,4},{7,5},{8,10},{9,11},{10,... | collective-permute-start | bytes 258056 | tf_op jit(solution)/shard_map/ppermute | solution.py:588
  (18 other events, 234.7 us)
